TPU v7x, 512 devices: a whole 4x4x16 slice. The times are simulated.
512 devices in a mesh: ev: 16 (over z), asset: 32 (over x, y, core).
Axes of the slice: x: 4, y: 4, z: 16, core: 2. Of those that a mesh axis runs over, the one named last changes fastest.
Arguments:
- hazard: bfloat16 [512, 163840], P('ev', 'asset'), may hold values from 0 to 1
- route_tiles: int32 [32, 64], P('asset'), may hold values from 0 to 4
- block_slots: int32 [4, 512], P(None, 'asset'), may hold values from 0 to 63, as said below
- corner_cells: int32 [4, 131072], P(None, 'asset'), may hold values from 0 to 4095
- corner_weights: float32 [4, 131072], P(None, 'asset'), may hold values from 0.05 to 1
- block_class: int32 [512], P('asset'), may hold values from 0 to 15
- curves: float32 [16, 16], replicated, may hold values from 0 to 1
- exposure: float32 [3, 131072], P(None, 'asset'), may hold values from 0.1 to 10
- event_ssp: int32 [512], P('ev'), may hold values from 0 to 2
- operator: bfloat16 [128, 131072], P('ev', 'asset'), may hold values from -0.03125 to 0.03125
Outputs:
- benefit: float32 [512, 128], P(('ev', 'asset'))
Inputs may be any that keep to these rules, and one draw needn't show every extreme that they name: `block_slots`: the 16 blocks of each device name each of its 64 slots.
All inputs are finite; a program needn't handle non-finite values.
Results may differ from a plain program's by a relative error of at most 0.0003.
Values may be sent and summed in bfloat16 or wider, within the bound.
No kernel may reach another device: no remote copies, remote signals or barrier semaphores. Data moves between devices by JAX's collectives and lax.ppermute only.
A program may use at most 64 MiB of HBM per device.

v0:
```python
import jax
import jax.numpy as jnp
from jax import lax
from jax.sharding import PartitionSpec as P

TILE = 1024
BLOCK = 256
OVL = 4
CORNERS = 4
SSPS = 3
CLASSES = 16
LEVELS = 16


def shards(
    hazard,
    route_tiles,
    block_slots,
    corner_cells,
    corner_weights,
    block_class,
    curves,
    exposure,
    event_ssp,
    operator,
):
    event_list = hazard.shape[0]
    devices = lax.axis_size("asset")
    slot_count = route_tiles.shape[1]
    pairwise_values = slot_count // devices
    tiles_dev = hazard.shape[1] // TILE
    whole, table = (
        lax.all_gather(hazard, "asset", axis=1, tiled=True),
        lax.all_gather(route_tiles, "asset", axis=0, tiled=True),
    )
    my_index = lax.axis_index("asset")
    mine = lax.dynamic_slice_in_dim(table, my_index * pairwise_values, pairwise_values, 1)
    tile_ids = (jnp.arange(devices, dtype=jnp.int32)[:, None] * tiles_dev + mine).reshape(-1)
    received = jnp.take(whole.reshape(event_list, devices * tiles_dev, TILE), tile_ids, axis=1)
    span = corner_cells.shape[1]
    block_count = span // BLOCK
    cell_range = jnp.arange(OVL * TILE, dtype=jnp.int32)
    block_cells = corner_cells.reshape(CORNERS, block_count, BLOCK).transpose(1, 0, 2)
    block_weights = corner_weights.reshape(CORNERS, block_count, BLOCK).transpose(1, 0, 2)

    def interpolate(items):
        slots_here, cells_here, weights_here = items
        window = jnp.take(received, slots_here, axis=1).reshape(event_list, OVL * TILE)
        weighted = jnp.zeros((event_list, BLOCK), jnp.float32)
        for corner in range(CORNERS):
            picker = (cells_here[corner][:, None] == cell_range[None, :]).astype(jnp.bfloat16)
            picked = lax.dot_general(
                window, picker, (((1,), (1,)), ((), ())), preferred_element_type=jnp.float32
            )
            weighted = weighted + weights_here[corner][None] * picked
        return weighted / jnp.sum(weights_here, axis=0)[None]

    per_block = lax.map(interpolate, (block_slots.T, block_cells, block_weights))
    hazard_intensity = per_block.transpose(1, 0, 2).reshape(event_list, span)
    onehot = (block_class[:, None] == jnp.arange(CLASSES, dtype=jnp.int32)[None, :]).astype(
        jnp.float32
    )
    block_curves = jnp.dot(onehot, curves, precision=lax.Precision.HIGHEST)
    asset_curves = jnp.repeat(block_curves, BLOCK, axis=0).T
    rescaled_values = (LEVELS - 1) * hazard_intensity
    ratio = jnp.zeros_like(hazard_intensity)
    for position in range(LEVELS):
        ratio = ratio + asset_curves[position][None] * jnp.maximum(
            0.0, 1.0 - jnp.abs(rescaled_values - position)
        )
    selected = jnp.zeros((event_list, span), jnp.float32)
    for scenario in range(SSPS):
        selected = jnp.where(event_ssp[:, None] == scenario, exposure[scenario][None, :], selected)
    impact = selected * ratio
    terms = lax.dot_general(
        impact,
        lax.all_gather(operator, "ev", axis=0, tiled=True).astype(jnp.float32),
        (((1,), (1,)), ((), ())),
        precision=lax.Precision.HIGHEST,
    )
    return lax.psum_scatter(terms, "asset", scatter_dimension=0, tiled=True)


def solution(mesh):
    in_specs = (
        P("ev", "asset"),
        P("asset", None),
        P(None, "asset"),
        P(None, "asset"),
        P(None, "asset"),
        P("asset"),
        P(),
        P(None, "asset"),
        P("ev"),
        P("ev", "asset"),
    )
    out_specs = P(("ev", "asset"), None)
    return jax.shard_map(shards, mesh=mesh, in_specs=in_specs, out_specs=out_specs, check_vma=False)
```

profile of v0, /device:TPU:1, one launch (start us, length us, event | category | flops | bytes accessed | tf_op | source)
XLA Modules:
  0.0 395.3 jit_solution(17126263731620728814)
XLA Ops:
  8.0 24.1 %all-gather = s32[32,1,64]{2,1,0:T(1,128)S(1)} all-gather(s32[1,1,64]{2,1,0:T(1,128)} %bitcast.243), channel_id=1, replica_groups=mesh['ev'=16,'asset'=32] {'asset'}, dimensions={0}, use_global_device_ids=true | all-gather | bytes 8448 | tf_op jit(solution)/shard_map/all_gather | solution.py:34
  37.7 51.7 %all-gather.4.cloned.1.call-done = bf16[32,163840]{1,0:T(8,128)(2,1)} async-done(((bf16[32,5120]{1,0:T(8,128)(2,1)}), bf16[32,163840]{1,0:T(8,128)(2,1)}) %all-gather.4.cloned.1.call-update) | async-done | bytes 10485776 | tf_op jit(solution)/shard_map/all_gather | solution.py:33
  89.5 9.7 %copy.106 = bf16[4,160,8,1024]{3,2,0,1:T(8,128)(2,1)} copy(bf16[4,160,8,1024]{3,2,1,0:T(8,128)(2,1)} %bitcast.186) | data formatting | bytes 20971520 | tf_op jit(solution)/shard_map/reshape | solution.py:39
  99.1 6.7 %gather_fusion.1 = bf16[64,32,1024]{2,1,0:T(8,128)(2,1)} fusion(bf16[32,160,1024]{2,0,1:T(8,128)(2,1)} %bitcast.185, s32[1024]{0:T(1024)S(1)} %pad_clamp_fusion.1), kind=kCustom, calls=%fused_computation.1 | custom fusion | bytes 8388864 | tf_op jit(solution)/shard_map/jit(_take)/gather | solution.py:39
  105.8 4.6 %select_bitcast_fusion = bf16[32,64,1024]{2,0,1:T(8,128)(2,1)} fusion(bf16[64,32,1024]{2,1,0:T(8,128)(2,1)} %gather_fusion.1, pred[64]{0:T(512)(128)(4,1)S(1)} %compare_and_fusion.1), kind=kLoop, calls=%fused_computation.52 | loop fusion | flops 2097152 | bytes 8388672 | tf_op jit(solution)/shard_map/jit(_take)/select_n | solution.py:39
  110.4 140.8 %while.13 = (s32[]{:T(128)}, f32[16,32,256]{2,1,0:T(8,128)S(1)}, f32[16,4,256]{2,1,0:T(4,128)}, s32[16,4]{1,0:T(8,128)S(1)}, bf16[32,64,1024]{2,0,1:T(8,128)(2,1)}, /*index=5*/s32[16,4,256]{2,1,0:T(4,128)}) while((s32[]{:T(128)}, f32[16,32,256]{2,1,0:T(8,128)S(1)}, f32[16,4,256]{2,1,0:T(4,128)}, ...), condition=%wide.region_2.3_spmd.clone.clone.clone, body=%wide.region_0.0_spmd.clone.clone.sunk.clone | while | flops 273221408 | bytes 2390265 | solution.py:58
  112.9 2.7 gather_fusion
  121.7 2.7 gather_fusion
  130.5 2.8 gather_fusion
  139.3 2.8 gather_fusion
  148.1 2.8 gather_fusion
  156.9 2.7 gather_fusion
  165.7 2.7 gather_fusion
  174.5 2.7 gather_fusion
  183.3 2.7 gather_fusion
  192.1 2.7 gather_fusion
  200.9 2.7 gather_fusion
  209.7 2.7 gather_fusion
  218.5 2.7 gather_fusion
  227.3 2.7 gather_fusion
  236.1 2.7 gather_fusion
  244.9 2.7 gather_fusion
  261.3 4.8 %fusion.29 = f32[32,128]{1,0:T(8,128)S(1)} fusion(bf16[128,4096]{1,0:T(8,128)(2,1)} %all-gather.6.cloned.1.call-done, f32[32,4096]{1,0:T(8,128)} %bitcast.206, f32[32,4096]{1,0:T(8,128)} %bitcast.205, f32[32,4096]{1,0:T(8,128)} %bitcast.204, f32[32,4096]{1,0:T(8,128)} %bitcast.203, f32[32,4096]{1,0:T(8,128)} %bitcast.202, f32[32,4096]{1,0:T(8,128)} %bitcast.201, ...), kind=kOutput, calls=%fused_computation.69 | convolution fusion | flops 205914112 | bytes 9764960 | tf_op jit(solution)/shard_map/dot_general | solution.py:75
  266.1 121.2 %all-reduce = f32[32,128]{1,0:T(8,128)S(1)} all-reduce(f32[32,128]{1,0:T(8,128)S(1)} %fusion.29), channel_id=2, replica_groups=mesh['ev'=16,'asset'=32] {'asset'}, use_global_device_ids=true, to_apply=%region_3.4.clone | all-reduce | flops 4096 | bytes 32768
  (252 shorter events, 113.7 us)
Async XLA Ops:
  6.5 28.5 %copy-start = (f32[16,16]{1,0:T(8,128)S(1)}, f32[16,16]{1,0:T(8,128)}, u32[]{:S(2)}) copy-start(f32[16,16]{1,0:T(8,128)} %param.18) | copy-start | bytes 3076
  6.5 82.9 %all-gather.4.cloned.1.call-start = ((), (), s32[]{:S(2)}) async-start(), calls=%async_computation | async-start | bytes 10813440 | tf_op jit(solution)/shard_map/all_gather | solution.py:33
  7.3 254.0 %all-gather.6.cloned.1.call-start = ((), (), s32[]{:S(2)}) async-start(), calls=%async_computation.1 | async-start | bytes 1114112 | tf_op jit(solution)/shard_map/all_gather | solution.py:77
Sparse Core Ops, SparseCore 0:
  10.5 78.8 all-gather.3
  91.5 61.1 all-gather.5
where the time goes:
time: 402 us; the launch traced here: 395 us
  blocking collectives  145 us (36%)
  local copies, waits for them, and re-layouts  103 us (26%)
  matrix products  60.8 us (15%)
  waiting for transfers between devices  53.1 us (13%)
  other arithmetic  18.4 us (5%)
  between operations  13.6 us (3%)
    unnamed x1, blocking collectives  121 us
    dot_general x64, matrix products, interpolate(): lax.dot_general(window, picker, (((1,), (1,)), ((), ())), preferred_eleme...  55.1 us
    all_gather x1, waiting for transfers between devices, shards(): lax.all_gather(hazard, 'asset', axis=1, tiled=True)  51.7 us
    gather x32, local copies, waits for them, and re-layouts, interpolate(): jnp.take(received, slots_here, axis=1).reshape(event_list, OVL * TILE)  44.3 us
    all_gather x1, blocking collectives, shards(): lax.all_gather(route_tiles, 'asset', axis=0, tiled=True)  24.1 us
    slice x16, local copies, waits for them, and re-layouts, interpolate(): cells_here[corner][:, None] == cell_range[None, :]  13.6 us
    slice x16, local copies, waits for them, and re-layouts, interpolate(): weighted = weighted + weights_here[corner][None] * picked  13.4 us
    reduce_sum x16, other arithmetic, interpolate(): return weighted / jnp.sum(weights_here, axis=0)[None]  11.3 us
  transfers between devices with their start and end apart: 2, of which 1 were waited for; matrix products, arithmetic and copies ran while one was open for 45% of the time, Pallas kernels for 0%

commit v1 on v0

v1 whole, which is shorter than its diff:
```python
import functools
import jax
import jax.numpy as jnp
from jax import lax
from jax.experimental import pallas as pl
from jax.experimental.pallas import tpu as pltpu
from jax.sharding import PartitionSpec as P

TILE = 1024
BLOCK = 256
OVL = 4
CORNERS = 4
SSPS = 3
CLASSES = 16
LEVELS = 16
LANES = 128
SUB = 8
DEPTH = 256


def pack_kernel(route_ref, hazard_ref, out_ref, sems):
    def copy(slot):
        first = pl.multiple_of(route_ref[0, slot] * TILE, TILE)
        return pltpu.make_async_copy(hazard_ref.at[:, pl.ds(first, TILE)], out_ref.at[slot], sems.at[slot])

    @pl.loop(0, out_ref.shape[0])
    def _(slot):
        copy(slot).start()

    @pl.loop(0, out_ref.shape[0])
    def _(slot):
        copy(slot).wait()


def pick_kernel(
    slots_ref, class_ref, tiles_ref, cells_ref, weights_ref, curves_ref, exposure_ref, ssp_ref, out_ref, window_ref, sems
):
    events = out_ref.shape[0]
    blocks = slots_ref.shape[1]
    pieces = TILE // DEPTH
    groups = events // SUB
    rows = lax.broadcasted_iota(jnp.int32, (DEPTH, BLOCK), 0)

    def fetch(block, k):
        at = lax.rem(block, 2)
        return pltpu.make_async_copy(tiles_ref.at[slots_ref[k, block]], window_ref.at[at, k], sems.at[at, k])

    for k in range(OVL):
        fetch(0, k).start()

    @pl.loop(0, blocks)
    def _(block):
        @pl.when(block + 1 < blocks)
        def _():
            for k in range(OVL):
                fetch(block + 1, k).start()

        for k in range(OVL):
            fetch(block, k).wait()
        at = lax.rem(block, 2)
        assets = pl.ds(pl.multiple_of(block * BLOCK, BLOCK), BLOCK)
        window = [
            window_ref[at, k, :, piece * DEPTH : (piece + 1) * DEPTH] for k in range(OVL) for piece in range(pieces)
        ]
        window = jnp.concatenate(window, axis=0)
        weights = [jnp.broadcast_to(weights_ref[pl.ds(at, 1), assets], (SUB, BLOCK)) for at in range(CORNERS)]
        scale = (LEVELS - 1) / (weights[0] + weights[1] + weights[2] + weights[3])
        place = [jnp.zeros((SUB, BLOCK), jnp.float32)] * groups
        for corner in range(CORNERS):
            cell = cells_ref[pl.ds(corner, 1), assets]
            picker = jnp.where(rows == (cell & (DEPTH - 1)), 1.0, 0.0).astype(jnp.bfloat16)
            found = jnp.dot(window, picker, preferred_element_type=jnp.float32)
            high = jnp.broadcast_to(cell, (SUB, BLOCK)) // DEPTH
            value = [found[group * SUB : (group + 1) * SUB] for group in range(groups)]
            for part in range(1, OVL * pieces):
                here = high == part
                for group in range(groups):
                    first = part * events + group * SUB
                    value[group] = jnp.where(here, found[first : first + SUB], value[group])
            place = [place[group] + weights[corner] * value[group] for group in range(groups)]
        row = class_ref[block]
        curve = jnp.broadcast_to(curves_ref[pl.ds(row, 1), :], (SUB, LANES))
        values = [jnp.broadcast_to(exposure_ref[pl.ds(at, 1), assets], (SUB, BLOCK)) for at in range(SSPS)]
        for group in range(groups):
            lines = slice(group * SUB, (group + 1) * SUB)
            spot = place[group] * scale
            level = jnp.clip(spot.astype(jnp.int32), 0, LEVELS - 2)
            part = spot - level.astype(jnp.float32)
            base, top = [], []
            for half in range(BLOCK // LANES):
                here = level[:, half * LANES : (half + 1) * LANES]
                base.append(jnp.take_along_axis(curve, here, axis=1, mode="promise_in_bounds"))
                top.append(jnp.take_along_axis(curve, here + 1, axis=1, mode="promise_in_bounds"))
            base, top = jnp.concatenate(base, axis=1), jnp.concatenate(top, axis=1)
            scenario = jnp.concatenate([ssp_ref[lines, :]] * (BLOCK // LANES), axis=1)
            value = jnp.where(scenario == 0, values[0], jnp.where(scenario == 1, values[1], values[2]))
            out_ref[lines, assets] = value * (base * (1.0 - part) + top * part)


def product_kernel(impact_ref, near_ref, far_ref, order_ref, out_ref):
    step = 512
    events, half = impact_ref.shape[0], near_ref.shape[0]
    dims = (((1,), (1,)), ((), ()))
    total = jnp.zeros((events, 2 * half), jnp.float32)
    for first in range(0, impact_ref.shape[1], step):
        impact = impact_ref[:, first : first + step]
        rows = jnp.concatenate([near_ref[:, first : first + step], far_ref[:, first : first + step]], axis=0)
        top = impact.astype(jnp.bfloat16)
        rest = (impact - top.astype(jnp.float32)).astype(jnp.bfloat16)
        both = jnp.concatenate([top, rest], axis=0)
        sums = lax.dot_general(both, rows, dims, preferred_element_type=jnp.float32)
        total = total + (sums[:events] + sums[events:])
    order = jnp.broadcast_to(order_ref[...], total.shape)
    out_ref[...] = jnp.take_along_axis(total, order, axis=1, mode="promise_in_bounds")


def vmem():
    return pl.BlockSpec(memory_space=pltpu.VMEM)


def smem():
    return pl.BlockSpec(memory_space=pltpu.SMEM)


def params():
    return pltpu.CompilerParams(vmem_limit_bytes=40 * 1024 * 1024)


def cost(flops, moved):
    return pl.CostEstimate(flops=flops, bytes_accessed=moved, transcendentals=0)


def shards(
    hazard,
    route_tiles,
    block_slots,
    corner_cells,
    corner_weights,
    block_class,
    curves,
    exposure,
    event_ssp,
    operator,
):
    events = hazard.shape[0]
    devices = lax.axis_size("asset")
    layers = lax.axis_size("ev")
    slots = route_tiles.shape[1]
    span = corner_cells.shape[1]
    with jax.named_scope("measures"):
        near = operator
        hops = []
        hop = layers // 2
        while hop:
            far = lax.ppermute(near, "ev", [(i, i ^ hop) for i in range(layers)])
            hops.append(hop)
            hop //= 2
            if hop:
                near = jnp.concatenate([near, far], axis=0)
        measures = operator.shape[0]
        owner = jnp.arange(layers * measures, dtype=jnp.int32) // measures ^ lax.axis_index("ev")
        place = sum(jnp.where(owner & hop, 1 << at, 0) for at, hop in enumerate(hops))
        order = place * measures + jnp.arange(layers * measures, dtype=jnp.int32) % measures
    with jax.named_scope("pack"):
        packed = pl.pallas_call(
            pack_kernel,
            out_shape=jax.ShapeDtypeStruct((slots, events, TILE), jnp.bfloat16),
            in_specs=[smem(), vmem()],
            out_specs=pl.BlockSpec(memory_space=pltpu.HBM),
            scratch_shapes=[pltpu.SemaphoreType.DMA((slots,))],
            compiler_params=params(),
            cost_estimate=cost(0, 8 * slots * events * TILE),
        )(route_tiles, hazard)
    with jax.named_scope("tiles"):
        tiles = lax.all_to_all(packed.reshape(devices, -1, TILE), "asset", 0, 0)
        tiles = tiles.reshape(slots, events, TILE)
    wide = jnp.pad(curves, ((0, 0), (0, LANES - LEVELS)))
    ssp = jnp.broadcast_to(event_ssp[:, None], (events, LANES))
    with jax.named_scope("pick"):
        impact = pl.pallas_call(
            pick_kernel,
            out_shape=jax.ShapeDtypeStruct((events, span), jnp.float32),
            in_specs=[smem(), smem(), pl.BlockSpec(memory_space=pl.ANY)] + [vmem()] * 5,
            out_specs=vmem(),
            scratch_shapes=[
                pltpu.VMEM((2, OVL, events, TILE), jnp.bfloat16),
                pltpu.SemaphoreType.DMA((2, OVL)),
            ],
            compiler_params=params(),
            cost_estimate=cost(2 * CORNERS * OVL * TILE * events * span, 2 * slots * events * TILE),
        )(block_slots, block_class, tiles, corner_cells, corner_weights, wide, exposure, ssp)
    with jax.named_scope("product"):
        terms = pl.pallas_call(
            product_kernel,
            out_shape=jax.ShapeDtypeStruct((events, order.shape[0]), jnp.float32),
            in_specs=[vmem()] * 4,
            out_specs=vmem(),
            compiler_params=params(),
            cost_estimate=cost(4 * events * order.shape[0] * span, 2 * order.shape[0] * span),
        )(impact, near, far, order[None])
    with jax.named_scope("sums"):
        parts = lax.all_to_all(terms[:, None, :], "asset", 0, 0)
        return jnp.sum(parts, axis=0)


def solution(mesh):
    in_specs = (
        P("ev", "asset"),
        P("asset", None),
        P(None, "asset"),
        P(None, "asset"),
        P(None, "asset"),
        P("asset"),
        P(),
        P(None, "asset"),
        P("ev"),
        P("ev", "asset"),
    )
    out_specs = P(("ev", "asset"), None)
    return jax.shard_map(shards, mesh=mesh, in_specs=in_specs, out_specs=out_specs, check_vma=False)
```

time: 402 us -> 100 us (0.25); the launches traced: 395 us -> 99.4 us
  blocking collectives: 145 us -> 13.9 us
  local copies, waits for them, and re-layouts: 103 us -> 3.75 us
  matrix products: 60.8 us -> 0 us
  starting transfers between devices: 0.04 us -> 33 us
  waiting for transfers between devices: 53.1 us -> 30.6 us
  other arithmetic: 18.4 us -> 0.61 us
  Pallas kernels: 0 us -> 17.4 us
  between operations: 13.6 us -> 0.2 us
    unnamed x1 -> x0, blocking collectives: 121 us -> none
    dot_general x66 -> x0, matrix products: 60.8 us -> none  [the longest x64 55.1 us: interpolate(): lax.dot_general(window, picker, (((1,), (1,)), ((), ())), preferred_eleme...]
    all_gather x2 -> x0, waiting for transfers between devices: 51.7 us -> none  [the longest x1 51.7 us: shards(): lax.all_gather(hazard, 'asset', axis=1, tiled=True)]
    gather x33 -> x0, local copies, waits for them, and re-layouts: 51 us -> none  [the longest x32 44.3 us: interpolate(): jnp.take(received, slots_here, axis=1).reshape(event_list, OVL * TILE)]
    ppermute x0 -> x4, waiting for transfers between devices: none -> 29.2 us  [shards(): far = lax.ppermute(near, 'ev', [(i, i ^ hop) for i in range(layers)])]
    slice x34 -> x0, local copies, waits for them, and re-layouts: 28.2 us -> none  [the longest x16 13.6 us: interpolate(): cells_here[corner][:, None] == cell_range[None, :]]
    all_gather x1 -> x0, blocking collectives: 24.1 us -> none  [shards(): lax.all_gather(route_tiles, 'asset', axis=0, tiled=True)]
    ppermute x0 -> x4, starting transfers between devices: none -> 21.5 us  [shards(): far = lax.ppermute(near, 'ev', [(i, i ^ hop) for i in range(layers)])]
  transfers between devices with their start and end apart: 2 -> 5, of which waited for: 1 -> 4; matrix products, arithmetic and copies ran while one was open for 45% -> 0% of each run, Pallas kernels for 0% -> 13%
where the time goes in v1:
time: 100 us; the launch traced here: 99.4 us
  starting transfers between devices  33 us (33%)
  waiting for transfers between devices  30.6 us (31%)
  Pallas kernels  17.4 us (17%)
  blocking collectives  13.9 us (14%)
  local copies, waits for them, and re-layouts  3.75 us (4%)
    ppermute x4, waiting for transfers between devices, shards(): far = lax.ppermute(near, 'ev', [(i, i ^ hop) for i in range(layers)])  29.2 us
    ppermute x4, starting transfers between devices, shards(): far = lax.ppermute(near, 'ev', [(i, i ^ hop) for i in range(layers)])  21.5 us
    all_to_all x1, blocking collectives, shards(): parts = lax.all_to_all(terms[:, None, :], 'asset', 0, 0)  13.9 us
    pallas_call x1, Pallas kernels, shards(): pl.pallas_call(pick_kernel, out_shape=jax.ShapeDtypeStruct((events, span)...  13.4 us
    all_to_all x1, starting transfers between devices, shards(): tiles = lax.all_to_all(packed.reshape(devices, -1, TILE), 'asset', 0, 0)  11.5 us
    unnamed x25, local copies, waits for them, and re-layouts  3.65 us
    pallas_call x1, Pallas kernels, shards(): pl.pallas_call(pack_kernel, out_shape=jax.ShapeDtypeStruct((slots, events...  3.5 us
  transfers between devices with their start and end apart: 5, of which 4 were waited for; matrix products, arithmetic and copies ran while one was open for 0% of the time, Pallas kernels for 13%

profile of v1, /device:TPU:1, one launch (start us, length us, event | category | flops | bytes accessed | tf_op | source)
XLA Modules:
  0.0 99.4 jit_solution(16914909913289532224)
XLA Ops:
  0.0 1.0 copy-done.1
  1.0 0.7 copy-done.2
  1.6 3.5 %pack.1 = bf16[64,32,1024]{2,1,0:T(8,128)(2,1)S(1)} custom-call(s32[1,64]{1,0:T(1,128)S(1)} %copy-done.2, bf16[32,5120]{1,0:T(8,128)(2,1)S(1)} %copy-done.1), custom_call_target="tpu_custom_call" | custom-call | bytes 16777216 | tf_op jit(solution)/shard_map/pack/pallas_call | solution.py:165
  5.1 0.0 copy-start
  5.1 2.0 %copy-done = bf16[64,32,1024]{2,1,0:T(8,128)(2,1)} copy-done((bf16[64,32,1024]{2,1,0:T(8,128)(2,1)}, bf16[64,32,1024]{2,1,0:T(8,128)(2,1)S(1)}, u32[]{:S(2)}) %copy-start) | copy-done | bytes 4194328
  7.1 0.0 copy-start.4
  7.1 0.0 copy-start.5
  7.1 0.0 copy-start.6
  7.2 0.0 copy-start.7
  7.2 11.5 %all-to-all-start = ((bf16[32,64,1024]{2,1,0:T(8,128)(2,1)}), bf16[32,64,1024]{2,1,0:T(8,128)(2,1)}, u32[]{:S(2)}, u32[]{:S(2)}) async-start(bf16[32,64,1024]{2,1,0:T(8,128)(2,1)} %bitcast.6), calls=%async_computation | async-start | bytes 8388608 | tf_op jit(solution)/shard_map/tiles/all_to_all | solution.py:175
  18.6 12.8 %collective-permute-start = (bf16[8,4096]{1,0:T(8,128)(2,1)S(1)}, bf16[8,4096]{1,0:T(8,128)(2,1)S(1)}, u32[]{:S(2)}, u32[]{:S(2)}) collective-permute-start(bf16[8,4096]{1,0:T(8,128)(2,1)S(1)} %copy-done.8), channel_id=1, source_target_pairs={{0,256},{32,288},{64,320},{96,352},{128,384},{160,416},{192,448},{... | collective-permute-start | bytes 196616 | tf_op jit(solution)/shard_map/measures/ppermute | solution.py:155
  31.4 2.2 %collective-permute-done = bf16[8,4096]{1,0:T(8,128)(2,1)S(1)} collective-permute-done((bf16[8,4096]{1,0:T(8,128)(2,1)S(1)}, bf16[8,4096]{1,0:T(8,128)(2,1)S(1)}, u32[]{:S(2)}, u32[]{:S(2)}) %collective-permute-start) | collective-permute-done | bytes 65568 | tf_op jit(solution)/shard_map/measures/ppermute | solution.py:155
  33.7 4.9 %collective-permute-start.1 = (bf16[16,4096]{1,0:T(8,128)(2,1)S(1)}, bf16[16,4096]{1,0:T(8,128)(2,1)S(1)}, u32[]{:S(2)}, u32[]{:S(2)}) collective-permute-start(bf16[16,4096]{1,0:T(8,128)(2,1)S(1)} %pad_maximum_fusion.1), channel_id=1, source_target_pairs={{0,128},{32,160},{64,192},{96,224},{128,0},{160,32},{192,64},{224,... | collective-permute-start | bytes 393224 | tf_op jit(solution)/shard_map/measures/ppermute | solution.py:155
  38.6 14.2 %collective-permute-done.1 = bf16[16,4096]{1,0:T(8,128)(2,1)S(1)} collective-permute-done((bf16[16,4096]{1,0:T(8,128)(2,1)S(1)}, bf16[16,4096]{1,0:T(8,128)(2,1)S(1)}, u32[]{:S(2)}, u32[]{:S(2)}) %collective-permute-start.1) | collective-permute-done | bytes 131104 | tf_op jit(solution)/shard_map/measures/ppermute | solution.py:155
  52.8 1.9 %collective-permute-start.2 = (bf16[32,4096]{1,0:T(8,128)(2,1)S(1)}, bf16[32,4096]{1,0:T(8,128)(2,1)S(1)}, u32[]{:S(2)}, u32[]{:S(2)}) collective-permute-start(bf16[32,4096]{1,0:T(8,128)(2,1)S(1)} %pad_maximum_fusion), channel_id=1, source_target_pairs={{0,64},{32,96},{64,0},{96,32},{128,192},{160,224},{192,128},{224,1... | collective-permute-start | bytes 786440 | tf_op jit(solution)/shard_map/measures/ppermute | solution.py:155
  54.7 12.8 %collective-permute-done.2 = bf16[32,4096]{1,0:T(8,128)(2,1)S(1)} collective-permute-done((bf16[32,4096]{1,0:T(8,128)(2,1)S(1)}, bf16[32,4096]{1,0:T(8,128)(2,1)S(1)}, u32[]{:S(2)}, u32[]{:S(2)}) %collective-permute-start.2) | collective-permute-done | bytes 262176 | tf_op jit(solution)/shard_map/measures/ppermute | solution.py:155
  67.6 1.9 %collective-permute-start.3 = (bf16[64,4096]{1,0:T(8,128)(2,1)S(1)}, bf16[64,4096]{1,0:T(8,128)(2,1)S(1)}, u32[]{:S(2)}, u32[]{:S(2)}) collective-permute-start(bf16[64,4096]{1,0:T(8,128)(2,1)S(1)} %constant_dynamic-update-slice_fusion.near_ref), channel_id=1, source_target_pairs={{0,32},{32,0},{64,96},{96,64},{128,160},{160,128},{192,224},{224,1... | collective-permute-start | bytes 1572872 | tf_op jit(solution)/shard_map/measures/ppermute | solution.py:155
  69.6 1.4 %all-to-all-done = bf16[32,64,1024]{2,1,0:T(8,128)(2,1)} async-done(((bf16[32,64,1024]{2,1,0:T(8,128)(2,1)}), bf16[32,64,1024]{2,1,0:T(8,128)(2,1)}, u32[]{:S(2)}, u32[]{:S(2)}) %all-to-all-start) | async-done | bytes 4194336 | tf_op jit(solution)/shard_map/tiles/all_to_all | solution.py:175
  70.9 0.1 broadcast_in_dim.22.ssp_ref
  71.0 13.4 %pick.1.impact_ref = f32[32,4096]{1,0:T(8,128)S(1)} custom-call(s32[4,16]{1,0:T(4,128)S(1)} %copy-done.6, s32[16]{0:T(128)S(1)} %copy-done.7, bf16[64,32,1024]{2,1,0:T(8,128)(2,1)} %bitcast.1.tiles_ref, s32[4,4096]{1,0:T(4,128)S(1)} %copy-done.3, f32[4,4096]{1,0:T(4,128)S(1)} %copy-done.4, f32[16,128]{1,0:T(8,128)S(1)} %pad.4.curves_ref, ...), custom_call_target="tpu_custom_call" | custom-call | flops 4294967296 | bytes 4194304 | tf_op jit(solution)/shard_map/pick/pallas_call | solution.py:180
  84.4 0.0 collective-permute-done.3.far_ref
  84.4 0.5 product.1
  85.0 13.9 %all_to_all.10 = f32[32,1,128]{2,1,0:T(1,128)S(1)} all-to-all(f32[32,1,128]{2,1,0:T(1,128)S(1)} %bitcast.7), channel_id=1, replica_groups=mesh['ev'=16,'asset'=32] {'asset'}, dimensions={0} | all-to-all | bytes 32768 | tf_op jit(solution)/shard_map/sums/all_to_all | solution.py:202
  98.8 0.6 reduce_sum.11
  (22 shorter events, 0.1 us)
Async XLA Ops:
  0.0 1.0 copy-start.1
  1.0 0.7 copy-start.2
  5.1 2.0 %copy-start = (bf16[64,32,1024]{2,1,0:T(8,128)(2,1)}, bf16[64,32,1024]{2,1,0:T(8,128)(2,1)S(1)}, u32[]{:S(2)}) copy-start(bf16[64,32,1024]{2,1,0:T(8,128)(2,1)S(1)} %pack.1) | copy-start | bytes 12582916
  7.1 11.5 %copy-start.8 = (bf16[8,4096]{1,0:T(8,128)(2,1)S(1)}, bf16[8,4096]{1,0:T(8,128)(2,1)}, u32[]{:S(2)}) copy-start(bf16[8,4096]{1,0:T(8,128)(2,1)} %param.19) | copy-start | bytes 196612
  7.1 62.4 %copy-start.9 = (f32[16,16]{1,0:T(8,128)S(1)}, f32[16,16]{1,0:T(8,128)}, u32[]{:S(2)}) copy-start(f32[16,16]{1,0:T(8,128)} %param.16) | copy-start | bytes 3076
  7.1 63.8 %copy-start.10 = (s32[32]{0:T(128)S(1)}, s32[32]{0:T(128)}, u32[]{:S(2)}) copy-start(s32[32]{0:T(128)} %param.18) | copy-start | bytes 388
  7.1 63.9 %copy-start.3 = (s32[4,4096]{1,0:T(4,128)S(1)}, s32[4,4096]{1,0:T(4,128)}, u32[]{:S(2)}) copy-start(s32[4,4096]{1,0:T(4,128)} %cells_ref.1) | copy-start | bytes 196612
  7.1 63.9 %copy-start.4 = (f32[4,4096]{1,0:T(4,128)S(1)}, f32[4,4096]{1,0:T(4,128)}, u32[]{:S(2)}) copy-start(f32[4,4096]{1,0:T(4,128)} %weights_ref.1) | copy-start | bytes 196612
  7.1 63.9 %copy-start.5 = (f32[3,4096]{1,0:T(4,128)S(1)}, f32[3,4096]{1,0:T(4,128)}, u32[]{:S(2)}) copy-start(f32[3,4096]{1,0:T(4,128)} %exposure_ref.1) | copy-start | bytes 147460
  7.1 63.9 %copy-start.6 = (s32[4,16]{1,0:T(4,128)S(1)}, s32[4,16]{1,0:T(4,128)}, u32[]{:S(2)}) copy-start(s32[4,16]{1,0:T(4,128)} %slots_ref.1) | copy-start | bytes 772
  7.2 63.9 %copy-start.7 = (s32[16]{0:T(128)S(1)}, s32[16]{0:T(128)}, u32[]{:S(2)}) copy-start(s32[16]{0:T(128)} %class_ref.1) | copy-start | bytes 196
  7.2 63.8 %all-to-all-start = ((bf16[32,64,1024]{2,1,0:T(8,128)(2,1)}), bf16[32,64,1024]{2,1,0:T(8,128)(2,1)}, u32[]{:S(2)}, u32[]{:S(2)}) async-start(bf16[32,64,1024]{2,1,0:T(8,128)(2,1)} %bitcast.6), calls=%async_computation | async-start | bytes 8388608 | tf_op jit(solution)/shard_map/tiles/all_to_all | solution.py:175
  18.6 15.0 %collective-permute-start = (bf16[8,4096]{1,0:T(8,128)(2,1)S(1)}, bf16[8,4096]{1,0:T(8,128)(2,1)S(1)}, u32[]{:S(2)}, u32[]{:S(2)}) collective-permute-start(bf16[8,4096]{1,0:T(8,128)(2,1)S(1)} %copy-done.8), channel_id=1, source_target_pairs={{0,256},{32,288},{64,320},{96,352},{128,384},{160,416},{192,448},{... | collective-permute-start | bytes 196616 | tf_op jit(solution)/shard_map/measures/ppermute | solution.py:155
  33.7 19.1 %collective-permute-start.1 = (bf16[16,4096]{1,0:T(8,128)(2,1)S(1)}, bf16[16,4096]{1,0:T(8,128)(2,1)S(1)}, u32[]{:S(2)}, u32[]{:S(2)}) collective-permute-start(bf16[16,4096]{1,0:T(8,128)(2,1)S(1)} %pad_maximum_fusion.1), channel_id=1, source_target_pairs={{0,128},{32,160},{64,192},{96,224},{128,0},{160,32},{192,64},{224,... | collective-permute-start | bytes 393224 | tf_op jit(solution)/shard_map/measures/ppermute | solution.py:155
  52.8 14.8 %collective-permute-start.2 = (bf16[32,4096]{1,0:T(8,128)(2,1)S(1)}, bf16[32,4096]{1,0:T(8,128)(2,1)S(1)}, u32[]{:S(2)}, u32[]{:S(2)}) collective-permute-start(bf16[32,4096]{1,0:T(8,128)(2,1)S(1)} %pad_maximum_fusion), channel_id=1, source_target_pairs={{0,64},{32,96},{64,0},{96,32},{128,192},{160,224},{192,128},{224,1... | collective-permute-start | bytes 786440 | tf_op jit(solution)/shard_map/measures/ppermute | solution.py:155
  67.6 16.8 %collective-permute-start.3 = (bf16[64,4096]{1,0:T(8,128)(2,1)S(1)}, bf16[64,4096]{1,0:T(8,128)(2,1)S(1)}, u32[]{:S(2)}, u32[]{:S(2)}) collective-permute-start(bf16[64,4096]{1,0:T(8,128)(2,1)S(1)} %constant_dynamic-update-slice_fusion.near_ref), channel_id=1, source_target_pairs={{0,32},{32,0},{64,96},{96,64},{128,160},{160,128},{192,224},{224,1... | collective-permute-start | bytes 1572872 | tf_op jit(solution)/shard_map/measures/ppermute | solution.py:155

commit v2 on v1

v2 whole, which is shorter than its diff:
```python
import functools
import jax
import jax.numpy as jnp
from jax import lax
from jax.experimental import pallas as pl
from jax.experimental.pallas import tpu as pltpu
from jax.sharding import PartitionSpec as P

TILE = 1024
BLOCK = 256
OVL = 4
CORNERS = 4
SSPS = 3
CLASSES = 16
LEVELS = 16
LANES = 128
SUB = 8
DEPTH = 256


def pack_kernel(routes_ref, tiles_ref, out_ref, route_ref, hazard_ref, first_sems, sems):
    route = pltpu.make_async_copy(routes_ref, route_ref, first_sems.at[0])
    hazard = pltpu.make_async_copy(tiles_ref, hazard_ref, first_sems.at[1])
    route.start()
    hazard.start()
    route.wait()
    hazard.wait()

    def copy(slot):
        first = pl.multiple_of(route_ref[0, slot] * TILE, TILE)
        return pltpu.make_async_copy(hazard_ref.at[:, pl.ds(first, TILE)], out_ref.at[slot], sems.at[slot])

    @pl.loop(0, out_ref.shape[0])
    def _(slot):
        copy(slot).start()

    @pl.loop(0, out_ref.shape[0])
    def _(slot):
        copy(slot).wait()


def pick_kernel(
    slots_ref, class_ref, tiles_ref, cells_ref, weights_ref, curves_ref, exposure_ref, ssp_ref, out_ref
):
    events = out_ref.shape[0]
    pieces = TILE // DEPTH
    groups = events // SUB
    rows = lax.broadcasted_iota(jnp.int32, (DEPTH, BLOCK), 0)

    @pl.loop(0, slots_ref.shape[1], unroll=4)
    def _(block):
        assets = pl.ds(pl.multiple_of(block * BLOCK, BLOCK), BLOCK)
        window = [
            tiles_ref[slots_ref[k, block], :, piece * DEPTH : (piece + 1) * DEPTH]
            for k in range(OVL)
            for piece in range(pieces)
        ]
        cells = [cells_ref[pl.ds(corner, 1), assets] for corner in range(CORNERS)]
        picker = [jnp.where(rows == (cell & (DEPTH - 1)), 1.0, 0.0).astype(jnp.bfloat16) for cell in cells]
        found = jnp.dot(
            jnp.concatenate(window, axis=0), jnp.concatenate(picker, axis=1), preferred_element_type=jnp.float32
        )
        weights = [jnp.broadcast_to(weights_ref[pl.ds(at, 1), assets], (SUB, BLOCK)) for at in range(CORNERS)]
        scale = (LEVELS - 1) / (weights[0] + weights[1] + weights[2] + weights[3])
        place = [jnp.zeros((SUB, BLOCK), jnp.float32)] * groups
        for corner in range(CORNERS):
            high = jnp.broadcast_to(cells[corner], (SUB, BLOCK)) // DEPTH
            mine = found[:, corner * BLOCK : (corner + 1) * BLOCK]
            value = [mine[group * SUB : (group + 1) * SUB] for group in range(groups)]
            for part in range(1, OVL * pieces):
                here = high == part
                for group in range(groups):
                    first = part * events + group * SUB
                    value[group] = jnp.where(here, mine[first : first + SUB], value[group])
            place = [place[group] + weights[corner] * value[group] for group in range(groups)]
        row = class_ref[block]
        curve = jnp.broadcast_to(curves_ref[pl.ds(row, 1), :], (SUB, LANES))
        values = [jnp.broadcast_to(exposure_ref[pl.ds(at, 1), assets], (SUB, BLOCK)) for at in range(SSPS)]
        for group in range(groups):
            lines = slice(group * SUB, (group + 1) * SUB)
            spot = place[group] * scale
            level = jnp.clip(spot.astype(jnp.int32), 0, LEVELS - 2)
            part = spot - level.astype(jnp.float32)
            base, top = [], []
            for half in range(BLOCK // LANES):
                here = level[:, half * LANES : (half + 1) * LANES]
                base.append(jnp.take_along_axis(curve, here, axis=1, mode="promise_in_bounds"))
                top.append(jnp.take_along_axis(curve, here + 1, axis=1, mode="promise_in_bounds"))
            base, top = jnp.concatenate(base, axis=1), jnp.concatenate(top, axis=1)
            scenario = jnp.concatenate([ssp_ref[lines, :]] * (BLOCK // LANES), axis=1)
            value = jnp.where(scenario == 0, values[0], jnp.where(scenario == 1, values[1], values[2]))
            out_ref[lines, assets] = value * (base * (1.0 - part) + top * part)


def product_kernel(impact_ref, order_ref, *refs):
    *rows_refs, out_ref = refs
    step = 512
    events = impact_ref.shape[0]
    dims = (((1,), (1,)), ((), ()))
    total = jnp.zeros(out_ref.shape, jnp.float32)
    for first in range(0, impact_ref.shape[1], step):
        impact = impact_ref[:, first : first + step]
        rows = jnp.concatenate([ref[:, first : first + step] for ref in rows_refs], axis=0)
        top = impact.astype(jnp.bfloat16)
        rest = (impact - top.astype(jnp.float32)).astype(jnp.bfloat16)
        both = jnp.concatenate([top, rest], axis=0)
        sums = lax.dot_general(both, rows, dims, preferred_element_type=jnp.float32)
        total = total + (sums[:events] + sums[events:])
    order = jnp.broadcast_to(order_ref[...], total.shape)
    out_ref[...] = jnp.take_along_axis(total, order, axis=1, mode="promise_in_bounds")


def vmem():
    return pl.BlockSpec(memory_space=pltpu.VMEM)


def smem():
    return pl.BlockSpec(memory_space=pltpu.SMEM)


def params():
    return pltpu.CompilerParams(vmem_limit_bytes=40 * 1024 * 1024)


def cost(flops, moved):
    return pl.CostEstimate(flops=flops, bytes_accessed=moved, transcendentals=0)


def measures_of(operator):
    layers = lax.axis_size("ev")
    measures = operator.shape[0]
    step = layers // 4

    def from_layer(rows, ahead):
        return lax.ppermute(rows, "ev", [((i + ahead) % layers, i) for i in range(layers)])

    far = [operator] + [from_layer(operator, ahead) for ahead in (step, 2 * step, 3 * step)]
    held = jnp.concatenate(far, axis=0)
    parts = [(held, [0, 1, 2, 3], 0)]
    for ahead in (1, -1):
        parts.append((from_layer(held, ahead), [0, 1, 2, 3], ahead))
    for ahead, blocks in ((2, (0, 1)), (-2, (3, 0))):
        some = jnp.concatenate([far[at] for at in blocks], axis=0)
        parts.append((from_layer(some, ahead), blocks, ahead))
    places = [(ahead + step * at) % layers for _, blocks, ahead in parts for at in blocks]
    measure = jnp.arange(layers * measures, dtype=jnp.int32)
    distance = (measure // measures - lax.axis_index("ev")) % layers
    place = sum(jnp.where(distance == far_off, at, 0) for at, far_off in enumerate(places))
    return [rows for rows, _, _ in parts], place * measures + measure % measures


def shards(
    hazard,
    route_tiles,
    block_slots,
    corner_cells,
    corner_weights,
    block_class,
    curves,
    exposure,
    event_ssp,
    operator,
):
    events = hazard.shape[0]
    devices = lax.axis_size("asset")
    slots = route_tiles.shape[1]
    span = corner_cells.shape[1]
    with jax.named_scope("measures"):
        parts, order = measures_of(operator)
    with jax.named_scope("pack"):
        packed = pl.pallas_call(
            pack_kernel,
            out_shape=pltpu.HBM((slots, events, TILE), jnp.bfloat16),
            in_specs=[pl.BlockSpec(memory_space=pltpu.HBM)] * 2,
            out_specs=pl.BlockSpec(memory_space=pltpu.HBM),
            scratch_shapes=[
                pltpu.SMEM((1, slots), jnp.int32),
                pltpu.VMEM(hazard.shape, hazard.dtype),
                pltpu.SemaphoreType.DMA((2,)),
                pltpu.SemaphoreType.DMA((slots,)),
            ],
            cost_estimate=cost(0, 8 * slots * events * TILE),
        )(route_tiles, hazard)
    with jax.named_scope("tiles"):
        tiles = lax.all_to_all(packed.reshape(devices, -1, TILE), "asset", 0, 0)
        tiles = tiles.reshape(slots, events, TILE)
    wide = jnp.pad(curves, ((0, 0), (0, LANES - LEVELS)))
    ssp = jnp.broadcast_to(event_ssp[:, None], (events, LANES))
    with jax.named_scope("pick"):
        impact = pl.pallas_call(
            pick_kernel,
            out_shape=jax.ShapeDtypeStruct((events, span), jnp.float32),
            in_specs=[smem(), smem()] + [vmem()] * 6,
            out_specs=vmem(),
            compiler_params=params(),
            cost_estimate=cost(2 * CORNERS * OVL * TILE * events * span, 2 * slots * events * TILE),
        )(block_slots, block_class, tiles, corner_cells, corner_weights, wide, exposure, ssp)
    with jax.named_scope("product"):
        terms = pl.pallas_call(
            product_kernel,
            out_shape=jax.ShapeDtypeStruct((events, order.shape[0]), jnp.float32),
            in_specs=[vmem()] * (2 + len(parts)),
            out_specs=vmem(),
            compiler_params=params(),
            cost_estimate=cost(4 * events * order.shape[0] * span, 2 * order.shape[0] * span),
        )(impact, order[None], *parts)
    with jax.named_scope("sums"):
        shares = lax.all_to_all(terms[:, None, :], "asset", 0, 0)
        return jnp.sum(shares, axis=0)


def solution(mesh):
    in_specs = (
        P("ev", "asset"),
        P("asset", None),
        P(None, "asset"),
        P(None, "asset"),
        P(None, "asset"),
        P("asset"),
        P(),
        P(None, "asset"),
        P("ev"),
        P("ev", "asset"),
    )
    out_specs = P(("ev", "asset"), None)
    return jax.shard_map(shards, mesh=mesh, in_specs=in_specs, out_specs=out_specs, check_vma=False)
```

time: 100 us -> 91.2 us (0.912)
  waiting for transfers between devices: 30.6 us -> 13.8 us
  starting transfers between devices: 33 us -> 49.7 us
  Pallas kernels: 17.4 us -> 12.3 us
  local copies, waits for them, and re-layouts: 3.75 us -> 0.15 us
    ppermute x4 -> x7, waiting for transfers between devices: 29.2 us -> 5.55 us  [from_layer(): lax.ppermute(rows, 'ev', [((i + ahead) % layers, i) for i in range(layers)])]
    ppermute x4 -> x7, starting transfers between devices: 21.5 us -> 38.3 us  [from_layer(): lax.ppermute(rows, 'ev', [((i + ahead) % layers, i) for i in range(layers)])]
    all_to_all x1, waiting for transfers between devices: 1.36 us -> 8.29 us  [shards(): tiles = lax.all_to_all(packed.reshape(devices, -1, TILE), 'asset', 0, 0)]
    pallas_call x1, Pallas kernels: 13.4 us -> 8.2 us  [shards(): pl.pallas_call(pick_kernel, out_shape=jax.ShapeDtypeStruct((events, span)...]
    unnamed x25 -> x19, local copies, waits for them, and re-layouts: 3.65 us -> 0.07 us
  transfers between devices with their start and end apart: 5 -> 8, of which waited for: 4 -> 3; matrix products, arithmetic and copies ran while one was open for 0% -> 0% of each run, Pallas kernels for 13% -> 9%
where the time goes in v2:
time: 91.2 us; the launch traced here: 90.7 us
  starting transfers between devices  49.7 us (54%)
  blocking collectives  13.9 us (15%)
  waiting for transfers between devices  13.8 us (15%)
  Pallas kernels  12.3 us (13%)
    ppermute x7, starting transfers between devices, from_layer(): lax.ppermute(rows, 'ev', [((i + ahead) % layers, i) for i in range(layers)])  38.3 us
    all_to_all x1, blocking collectives, shards(): shares = lax.all_to_all(terms[:, None, :], 'asset', 0, 0)  13.9 us
    all_to_all x1, starting transfers between devices, shards(): tiles = lax.all_to_all(packed.reshape(devices, -1, TILE), 'asset', 0, 0)  11.5 us
    all_to_all x1, waiting for transfers between devices, shards(): tiles = lax.all_to_all(packed.reshape(devices, -1, TILE), 'asset', 0, 0)  8.29 us
    pallas_call x1, Pallas kernels, shards(): pl.pallas_call(pick_kernel, out_shape=jax.ShapeDtypeStruct((events, span)...  8.2 us
    ppermute x7, waiting for transfers between devices, from_layer(): lax.ppermute(rows, 'ev', [((i + ahead) % layers, i) for i in range(layers)])  5.55 us
    pallas_call x1, Pallas kernels, shards(): pl.pallas_call(pack_kernel, out_shape=pltpu.HBM((slots, events, TILE), jn...  3.52 us
  transfers between devices with their start and end apart: 8, of which 3 were waited for; matrix products, arithmetic and copies ran while one was open for 0% of the time, Pallas kernels for 9%

profile of v2, /device:TPU:1, one launch (start us, length us, event | category | flops | bytes accessed | tf_op | source)
XLA Modules:
  0.0 90.7 jit_solution(14674219022466732529)
XLA Ops:
  0.0 3.5 %pack.1 = bf16[64,32,1024]{2,1,0:T(8,128)(2,1)} custom-call(s32[1,64]{1,0:T(1,128)} %routes_ref.1, bf16[32,5120]{1,0:T(8,128)(2,1)} %tiles_ref.1), custom_call_target="tpu_custom_call" | custom-call | bytes 16777216 | tf_op jit(solution)/shard_map/pack/pallas_call | solution.py:171
  3.5 0.0 copy-start.5
  3.5 0.0 copy-start.6
  3.6 0.0 copy-start.7
  3.6 0.0 copy-start
  3.6 0.0 copy-start.1
  3.6 0.0 copy-start.3
  3.6 0.0 copy-start.4
  3.6 11.5 %all-to-all-start = ((bf16[32,64,1024]{2,1,0:T(8,128)(2,1)}), bf16[32,64,1024]{2,1,0:T(8,128)(2,1)}, u32[]{:S(2)}, u32[]{:S(2)}) async-start(bf16[32,64,1024]{2,1,0:T(8,128)(2,1)} %bitcast.7), calls=%async_computation | async-start | bytes 8388608 | tf_op jit(solution)/shard_map/tiles/all_to_all | solution.py:185
  15.1 9.8 %collective-permute-start = (bf16[8,4096]{1,0:T(8,128)(2,1)S(1)}, bf16[8,4096]{1,0:T(8,128)(2,1)S(1)}, u32[]{:S(2)}, u32[]{:S(2)}) collective-permute-start(bf16[8,4096]{1,0:T(8,128)(2,1)S(1)} %copy-done.5), channel_id=1, source_target_pairs={{128,0},{160,32},{192,64},{224,96},{256,128},{288,160},{320,192},{... | collective-permute-start | bytes 196616 | tf_op jit(solution)/shard_map/measures/ppermute | solution.py:135
  24.9 4.9 %collective-permute-start.1 = (bf16[8,4096]{1,0:T(8,128)(2,1)S(1)}, bf16[8,4096]{1,0:T(8,128)(2,1)S(1)}, u32[]{:S(2)}, u32[]{:S(2)}) collective-permute-start(bf16[8,4096]{1,0:T(8,128)(2,1)S(1)} %copy-done.5), channel_id=1, source_target_pairs={{256,0},{288,32},{320,64},{352,96},{384,128},{416,160},{448,192},{... | collective-permute-start | bytes 196616 | tf_op jit(solution)/shard_map/measures/ppermute | solution.py:135
  29.8 7.3 %collective-permute-start.2 = (bf16[8,4096]{1,0:T(8,128)(2,1)S(1)}, bf16[8,4096]{1,0:T(8,128)(2,1)S(1)}, u32[]{:S(2)}, u32[]{:S(2)}) collective-permute-start(bf16[8,4096]{1,0:T(8,128)(2,1)S(1)} %copy-done.5), channel_id=1, source_target_pairs={{384,0},{416,32},{448,64},{480,96},{0,128},{32,160},{64,192},{96,2... | collective-permute-start | bytes 196616 | tf_op jit(solution)/shard_map/measures/ppermute | solution.py:135
  37.2 1.8 %collective-permute-done.1 = bf16[8,4096]{1,0:T(8,128)(2,1)S(1)} collective-permute-done((bf16[8,4096]{1,0:T(8,128)(2,1)S(1)}, bf16[8,4096]{1,0:T(8,128)(2,1)S(1)}, u32[]{:S(2)}, u32[]{:S(2)}) %collective-permute-start.1) | collective-permute-done | bytes 65568 | tf_op jit(solution)/shard_map/measures/ppermute | solution.py:135
  39.0 3.8 %collective-permute-done.2 = bf16[8,4096]{1,0:T(8,128)(2,1)S(1)} collective-permute-done((bf16[8,4096]{1,0:T(8,128)(2,1)S(1)}, bf16[8,4096]{1,0:T(8,128)(2,1)S(1)}, u32[]{:S(2)}, u32[]{:S(2)}) %collective-permute-start.2) | collective-permute-done | bytes 65568 | tf_op jit(solution)/shard_map/measures/ppermute | solution.py:135
  42.7 8.2 %collective-permute-start.3 = (bf16[32,4096]{1,0:T(8,128)(2,1)S(1)}, bf16[32,4096]{1,0:T(8,128)(2,1)S(1)}, u32[]{:S(2)}, u32[]{:S(2)}) collective-permute-start(bf16[32,4096]{1,0:T(8,128)(2,1)S(1)} %constant_dynamic-update-slice_fusion.refs_0_), channel_id=1, source_target_pairs={{32,0},{64,32},{96,64},{128,96},{160,128},{192,160},{224,192},{256... | collective-permute-start | bytes 786440 | tf_op jit(solution)/shard_map/measures/ppermute | solution.py:135
  51.0 1.9 %collective-permute-start.4 = (bf16[32,4096]{1,0:T(8,128)(2,1)S(1)}, bf16[32,4096]{1,0:T(8,128)(2,1)S(1)}, u32[]{:S(2)}, u32[]{:S(2)}) collective-permute-start(bf16[32,4096]{1,0:T(8,128)(2,1)S(1)} %constant_dynamic-update-slice_fusion.refs_0_), channel_id=1, source_target_pairs={{480,0},{0,32},{32,64},{64,96},{96,128},{128,160},{160,192},{192,2... | collective-permute-start | bytes 786440 | tf_op jit(solution)/shard_map/measures/ppermute | solution.py:135
  52.9 3.1 %collective-permute-start.5 = (bf16[16,4096]{1,0:T(8,128)(2,1)S(1)}, bf16[16,4096]{1,0:T(8,128)(2,1)S(1)}, u32[]{:S(2)}, u32[]{:S(2)}) collective-permute-start(bf16[16,4096]{1,0:T(8,128)(2,1)S(1)} %get-tuple-element.6), channel_id=1, source_target_pairs={{64,0},{96,32},{128,64},{160,96},{192,128},{224,160},{256,192},{28... | collective-permute-start | bytes 393224 | tf_op jit(solution)/shard_map/measures/ppermute | solution.py:135
  56.0 3.1 %collective-permute-start.6 = (bf16[16,4096]{1,0:T(8,128)(2,1)S(1)}, bf16[16,4096]{1,0:T(8,128)(2,1)S(1)}, u32[]{:S(2)}, u32[]{:S(2)}) collective-permute-start(bf16[16,4096]{1,0:T(8,128)(2,1)S(1)} %get-tuple-element.5), channel_id=1, source_target_pairs={{448,0},{480,32},{0,64},{32,96},{64,128},{96,160},{128,192},{160,2... | collective-permute-start | bytes 393224 | tf_op jit(solution)/shard_map/measures/ppermute | solution.py:135
  59.1 8.3 %all-to-all-done = bf16[32,64,1024]{2,1,0:T(8,128)(2,1)} async-done(((bf16[32,64,1024]{2,1,0:T(8,128)(2,1)}), bf16[32,64,1024]{2,1,0:T(8,128)(2,1)}, u32[]{:S(2)}, u32[]{:S(2)}) %all-to-all-start) | async-done | bytes 4194336 | tf_op jit(solution)/shard_map/tiles/all_to_all | solution.py:185
  67.4 0.1 broadcast_in_dim.52.ssp_ref
  67.5 8.2 %pick.1.impact_ref = f32[32,4096]{1,0:T(8,128)S(1)} custom-call(s32[4,16]{1,0:T(4,128)S(1)} %copy-done.3, s32[16]{0:T(128)S(1)} %copy-done.4, bf16[64,32,1024]{2,1,0:T(8,128)(2,1)} %bitcast.1.tiles_ref, s32[4,4096]{1,0:T(4,128)S(1)} %copy-done, f32[4,4096]{1,0:T(4,128)S(1)} %copy-done.1, f32[16,128]{1,0:T(8,128)S(1)} %pad.4.curves_ref, ...), custom_call_target="tpu_custom_call" | custom-call | flops 4294967296 | bytes 4194304 | tf_op jit(solution)/shard_map/pick/pallas_call | solution.py:190
  75.7 0.5 product.1
  76.3 13.9 %all_to_all.10 = f32[32,1,128]{2,1,0:T(1,128)S(1)} all-to-all(f32[32,1,128]{2,1,0:T(1,128)S(1)} %bitcast.6), channel_id=1, replica_groups=mesh['ev'=16,'asset'=32] {'asset'}, dimensions={0} | all-to-all | bytes 32768 | tf_op jit(solution)/shard_map/sums/all_to_all | solution.py:208
  90.2 0.6 reduce_sum.11
  (21 shorter events, 0.1 us)
Async XLA Ops:
  3.5 11.6 %copy-start.5 = (bf16[8,4096]{1,0:T(8,128)(2,1)S(1)}, bf16[8,4096]{1,0:T(8,128)(2,1)}, u32[]{:S(2)}) copy-start(bf16[8,4096]{1,0:T(8,128)(2,1)} %param.19) | copy-start | bytes 196612
  3.5 33.6 %copy-start.6 = (f32[16,16]{1,0:T(8,128)S(1)}, f32[16,16]{1,0:T(8,128)}, u32[]{:S(2)}) copy-start(f32[16,16]{1,0:T(8,128)} %param.16) | copy-start | bytes 3076
  3.6 63.8 %copy-start.7 = (s32[32]{0:T(128)S(1)}, s32[32]{0:T(128)}, u32[]{:S(2)}) copy-start(s32[32]{0:T(128)} %param.18) | copy-start | bytes 388
  3.6 63.9 %copy-start = (s32[4,4096]{1,0:T(4,128)S(1)}, s32[4,4096]{1,0:T(4,128)}, u32[]{:S(2)}) copy-start(s32[4,4096]{1,0:T(4,128)} %cells_ref.1) | copy-start | bytes 196612
  3.6 63.9 %copy-start.1 = (f32[4,4096]{1,0:T(4,128)S(1)}, f32[4,4096]{1,0:T(4,128)}, u32[]{:S(2)}) copy-start(f32[4,4096]{1,0:T(4,128)} %weights_ref.1) | copy-start | bytes 196612
  3.6 63.9 %copy-start.2 = (f32[3,4096]{1,0:T(4,128)S(1)}, f32[3,4096]{1,0:T(4,128)}, u32[]{:S(2)}) copy-start(f32[3,4096]{1,0:T(4,128)} %exposure_ref.1) | copy-start | bytes 147460
  3.6 63.9 %copy-start.3 = (s32[4,16]{1,0:T(4,128)S(1)}, s32[4,16]{1,0:T(4,128)}, u32[]{:S(2)}) copy-start(s32[4,16]{1,0:T(4,128)} %slots_ref.1) | copy-start | bytes 772
  3.6 63.9 %copy-start.4 = (s32[16]{0:T(128)S(1)}, s32[16]{0:T(128)}, u32[]{:S(2)}) copy-start(s32[16]{0:T(128)} %class_ref.1) | copy-start | bytes 196
  3.6 63.8 %all-to-all-start = ((bf16[32,64,1024]{2,1,0:T(8,128)(2,1)}), bf16[32,64,1024]{2,1,0:T(8,128)(2,1)}, u32[]{:S(2)}, u32[]{:S(2)}) async-start(bf16[32,64,1024]{2,1,0:T(8,128)(2,1)} %bitcast.7), calls=%async_computation | async-start | bytes 8388608 | tf_op jit(solution)/shard_map/tiles/all_to_all | solution.py:185
  15.1 22.1 %collective-permute-start = (bf16[8,4096]{1,0:T(8,128)(2,1)S(1)}, bf16[8,4096]{1,0:T(8,128)(2,1)S(1)}, u32[]{:S(2)}, u32[]{:S(2)}) collective-permute-start(bf16[8,4096]{1,0:T(8,128)(2,1)S(1)} %copy-done.5), channel_id=1, source_target_pairs={{128,0},{160,32},{192,64},{224,96},{256,128},{288,160},{320,192},{... | collective-permute-start | bytes 196616 | tf_op jit(solution)/shard_map/measures/ppermute | solution.py:135
  24.9 14.0 %collective-permute-start.1 = (bf16[8,4096]{1,0:T(8,128)(2,1)S(1)}, bf16[8,4096]{1,0:T(8,128)(2,1)S(1)}, u32[]{:S(2)}, u32[]{:S(2)}) collective-permute-start(bf16[8,4096]{1,0:T(8,128)(2,1)S(1)} %copy-done.5), channel_id=1, source_target_pairs={{256,0},{288,32},{320,64},{352,96},{384,128},{416,160},{448,192},{... | collective-permute-start | bytes 196616 | tf_op jit(solution)/shard_map/measures/ppermute | solution.py:135
  29.8 12.9 %collective-permute-start.2 = (bf16[8,4096]{1,0:T(8,128)(2,1)S(1)}, bf16[8,4096]{1,0:T(8,128)(2,1)S(1)}, u32[]{:S(2)}, u32[]{:S(2)}) collective-permute-start(bf16[8,4096]{1,0:T(8,128)(2,1)S(1)} %copy-done.5), channel_id=1, source_target_pairs={{384,0},{416,32},{448,64},{480,96},{0,128},{32,160},{64,192},{96,2... | collective-permute-start | bytes 196616 | tf_op jit(solution)/shard_map/measures/ppermute | solution.py:135
  42.7 33.0 %collective-permute-start.3 = (bf16[32,4096]{1,0:T(8,128)(2,1)S(1)}, bf16[32,4096]{1,0:T(8,128)(2,1)S(1)}, u32[]{:S(2)}, u32[]{:S(2)}) collective-permute-start(bf16[32,4096]{1,0:T(8,128)(2,1)S(1)} %constant_dynamic-update-slice_fusion.refs_0_), channel_id=1, source_target_pairs={{32,0},{64,32},{96,64},{128,96},{160,128},{192,160},{224,192},{256... | collective-permute-start | bytes 786440 | tf_op jit(solution)/shard_map/measures/ppermute | solution.py:135
  51.0 24.8 %collective-permute-start.4 = (bf16[32,4096]{1,0:T(8,128)(2,1)S(1)}, bf16[32,4096]{1,0:T(8,128)(2,1)S(1)}, u32[]{:S(2)}, u32[]{:S(2)}) collective-permute-start(bf16[32,4096]{1,0:T(8,128)(2,1)S(1)} %constant_dynamic-update-slice_fusion.refs_0_), channel_id=1, source_target_pairs={{480,0},{0,32},{32,64},{64,96},{96,128},{128,160},{160,192},{192,2... | collective-permute-start | bytes 786440 | tf_op jit(solution)/shard_map/measures/ppermute | solution.py:135
  52.9 22.8 %collective-permute-start.5 = (bf16[16,4096]{1,0:T(8,128)(2,1)S(1)}, bf16[16,4096]{1,0:T(8,128)(2,1)S(1)}, u32[]{:S(2)}, u32[]{:S(2)}) collective-permute-start(bf16[16,4096]{1,0:T(8,128)(2,1)S(1)} %get-tuple-element.6), channel_id=1, source_target_pairs={{64,0},{96,32},{128,64},{160,96},{192,128},{224,160},{256,192},{28... | collective-permute-start | bytes 393224 | tf_op jit(solution)/shard_map/measures/ppermute | solution.py:135
  56.0 19.7 %collective-permute-start.6 = (bf16[16,4096]{1,0:T(8,128)(2,1)S(1)}, bf16[16,4096]{1,0:T(8,128)(2,1)S(1)}, u32[]{:S(2)}, u32[]{:S(2)}) collective-permute-start(bf16[16,4096]{1,0:T(8,128)(2,1)S(1)} %get-tuple-element.5), channel_id=1, source_target_pairs={{448,0},{480,32},{0,64},{32,96},{64,128},{96,160},{128,192},{160,2... | collective-permute-start | bytes 393224 | tf_op jit(solution)/shard_map/measures/ppermute | solution.py:135

commit v3 on v2

--- a/solution.py
+++ b/solution.py
@@ -16,6 +16,7 @@
 LANES = 128
 SUB = 8
 DEPTH = 256
+PACK = 16
 
 
 def pack_kernel(routes_ref, tiles_ref, out_ref, route_ref, hazard_ref, first_sems, sems):
@@ -45,9 +46,17 @@
     events = out_ref.shape[0]
     pieces = TILE // DEPTH
     groups = events // SUB
-    rows = lax.broadcasted_iota(jnp.int32, (DEPTH, BLOCK), 0)
-
-    @pl.loop(0, slots_ref.shape[1], unroll=4)
+    rows = lax.broadcasted_iota(jnp.int32, (DEPTH, BLOCK), 0).astype(jnp.float32).astype(jnp.bfloat16)
+
+    def one_hot(cell):
+        low = jnp.broadcast_to((cell & (DEPTH - 1)).astype(jnp.float32), (PACK, BLOCK)).astype(jnp.bfloat16)
+        hits = [
+            jnp.where(rows[first : first + PACK] == low, jnp.bfloat16(1), jnp.bfloat16(0))
+            for first in range(0, DEPTH, PACK)
+        ]
+        return jnp.concatenate(hits, axis=0)
+
+    @pl.loop(0, slots_ref.shape[1], unroll=8)
     def _(block):
         assets = pl.ds(pl.multiple_of(block * BLOCK, BLOCK), BLOCK)
         window = [
@@ -56,10 +65,8 @@
             for piece in range(pieces)
         ]
         cells = [cells_ref[pl.ds(corner, 1), assets] for corner in range(CORNERS)]
-        picker = [jnp.where(rows == (cell & (DEPTH - 1)), 1.0, 0.0).astype(jnp.bfloat16) for cell in cells]
-        found = jnp.dot(
-            jnp.concatenate(window, axis=0), jnp.concatenate(picker, axis=1), preferred_element_type=jnp.float32
-        )
+        picker = jnp.concatenate([one_hot(cell) for cell in cells], axis=1)
+        found = jnp.dot(jnp.concatenate(window, axis=0), picker, preferred_element_type=jnp.float32)
         weights = [jnp.broadcast_to(weights_ref[pl.ds(at, 1), assets], (SUB, BLOCK)) for at in range(CORNERS)]
         scale = (LEVELS - 1) / (weights[0] + weights[1] + weights[2] + weights[3])
         place = [jnp.zeros((SUB, BLOCK), jnp.float32)] * groups

time: 91.2 us -> 90.2 us (0.989)
  Pallas kernels: 12.3 us -> 11.3 us
    pallas_call x1, Pallas kernels: 8.2 us -> 7.2 us  [shards(): pl.pallas_call(pick_kernel, out_shape=jax.ShapeDtypeStruct((events, span)...]
  transfers between devices with their start and end apart: 8 -> 8, of which waited for: 3 -> 3; matrix products, arithmetic and copies ran while one was open for 0% -> 0% of each run, Pallas kernels for 9% -> 8%
where the time goes in v3:
time: 90.2 us; the launch traced here: 89.7 us
  starting transfers between devices  49.7 us (55%)
  blocking collectives  13.9 us (15%)
  waiting for transfers between devices  13.8 us (15%)
  Pallas kernels  11.3 us (13%)
    ppermute x7, starting transfers between devices, from_layer(): lax.ppermute(rows, 'ev', [((i + ahead) % layers, i) for i in range(layers)])  38.3 us
    all_to_all x1, blocking collectives, shards(): shares = lax.all_to_all(terms[:, None, :], 'asset', 0, 0)  13.9 us
    all_to_all x1, starting transfers between devices, shards(): tiles = lax.all_to_all(packed.reshape(devices, -1, TILE), 'asset', 0, 0)  11.5 us
    all_to_all x1, waiting for transfers between devices, shards(): tiles = lax.all_to_all(packed.reshape(devices, -1, TILE), 'asset', 0, 0)  8.29 us
    pallas_call x1, Pallas kernels, shards(): pl.pallas_call(pick_kernel, out_shape=jax.ShapeDtypeStruct((events, span)...  7.2 us
    ppermute x7, waiting for transfers between devices, from_layer(): lax.ppermute(rows, 'ev', [((i + ahead) % layers, i) for i in range(layers)])  5.55 us
    pallas_call x1, Pallas kernels, shards(): pl.pallas_call(pack_kernel, out_shape=pltpu.HBM((slots, events, TILE), jn...  3.52 us
  transfers between devices with their start and end apart: 8, of which 3 were waited for; matrix products, arithmetic and copies ran while one was open for 0% of the time, Pallas kernels for 8%

profile of v3, /device:TPU:1, one launch (start us, length us, event | category | flops | bytes accessed | tf_op | source)
XLA Modules:
  0.0 89.7 jit_solution(17044381579013220188)
XLA Ops:
  0.0 3.5 %pack.1 = bf16[64,32,1024]{2,1,0:T(8,128)(2,1)} custom-call(s32[1,64]{1,0:T(1,128)} %routes_ref.1, bf16[32,5120]{1,0:T(8,128)(2,1)} %tiles_ref.1), custom_call_target="tpu_custom_call" | custom-call | bytes 16777216 | tf_op jit(solution)/shard_map/pack/pallas_call | solution.py:178
  3.5 0.0 copy-start.5
  3.5 0.0 copy-start.6
  3.6 0.0 copy-start.7
  3.6 0.0 copy-start
  3.6 0.0 copy-start.1
  3.6 0.0 copy-start.3
  3.6 0.0 copy-start.4
  3.6 11.5 %all-to-all-start = ((bf16[32,64,1024]{2,1,0:T(8,128)(2,1)}), bf16[32,64,1024]{2,1,0:T(8,128)(2,1)}, u32[]{:S(2)}, u32[]{:S(2)}) async-start(bf16[32,64,1024]{2,1,0:T(8,128)(2,1)} %bitcast.7), calls=%async_computation | async-start | bytes 8388608 | tf_op jit(solution)/shard_map/tiles/all_to_all | solution.py:192
  15.1 9.8 %collective-permute-start = (bf16[8,4096]{1,0:T(8,128)(2,1)S(1)}, bf16[8,4096]{1,0:T(8,128)(2,1)S(1)}, u32[]{:S(2)}, u32[]{:S(2)}) collective-permute-start(bf16[8,4096]{1,0:T(8,128)(2,1)S(1)} %copy-done.5), channel_id=1, source_target_pairs={{128,0},{160,32},{192,64},{224,96},{256,128},{288,160},{320,192},{... | collective-permute-start | bytes 196616 | tf_op jit(solution)/shard_map/measures/ppermute | solution.py:142
  24.9 4.9 %collective-permute-start.1 = (bf16[8,4096]{1,0:T(8,128)(2,1)S(1)}, bf16[8,4096]{1,0:T(8,128)(2,1)S(1)}, u32[]{:S(2)}, u32[]{:S(2)}) collective-permute-start(bf16[8,4096]{1,0:T(8,128)(2,1)S(1)} %copy-done.5), channel_id=1, source_target_pairs={{256,0},{288,32},{320,64},{352,96},{384,128},{416,160},{448,192},{... | collective-permute-start | bytes 196616 | tf_op jit(solution)/shard_map/measures/ppermute | solution.py:142
  29.8 7.3 %collective-permute-start.2 = (bf16[8,4096]{1,0:T(8,128)(2,1)S(1)}, bf16[8,4096]{1,0:T(8,128)(2,1)S(1)}, u32[]{:S(2)}, u32[]{:S(2)}) collective-permute-start(bf16[8,4096]{1,0:T(8,128)(2,1)S(1)} %copy-done.5), channel_id=1, source_target_pairs={{384,0},{416,32},{448,64},{480,96},{0,128},{32,160},{64,192},{96,2... | collective-permute-start | bytes 196616 | tf_op jit(solution)/shard_map/measures/ppermute | solution.py:142
  37.2 1.8 %collective-permute-done.1 = bf16[8,4096]{1,0:T(8,128)(2,1)S(1)} collective-permute-done((bf16[8,4096]{1,0:T(8,128)(2,1)S(1)}, bf16[8,4096]{1,0:T(8,128)(2,1)S(1)}, u32[]{:S(2)}, u32[]{:S(2)}) %collective-permute-start.1) | collective-permute-done | bytes 65568 | tf_op jit(solution)/shard_map/measures/ppermute | solution.py:142
  39.0 3.8 %collective-permute-done.2 = bf16[8,4096]{1,0:T(8,128)(2,1)S(1)} collective-permute-done((bf16[8,4096]{1,0:T(8,128)(2,1)S(1)}, bf16[8,4096]{1,0:T(8,128)(2,1)S(1)}, u32[]{:S(2)}, u32[]{:S(2)}) %collective-permute-start.2) | collective-permute-done | bytes 65568 | tf_op jit(solution)/shard_map/measures/ppermute | solution.py:142
  42.7 8.2 %collective-permute-start.3 = (bf16[32,4096]{1,0:T(8,128)(2,1)S(1)}, bf16[32,4096]{1,0:T(8,128)(2,1)S(1)}, u32[]{:S(2)}, u32[]{:S(2)}) collective-permute-start(bf16[32,4096]{1,0:T(8,128)(2,1)S(1)} %constant_dynamic-update-slice_fusion.refs_0_), channel_id=1, source_target_pairs={{32,0},{64,32},{96,64},{128,96},{160,128},{192,160},{224,192},{256... | collective-permute-start | bytes 786440 | tf_op jit(solution)/shard_map/measures/ppermute | solution.py:142
  51.0 1.9 %collective-permute-start.4 = (bf16[32,4096]{1,0:T(8,128)(2,1)S(1)}, bf16[32,4096]{1,0:T(8,128)(2,1)S(1)}, u32[]{:S(2)}, u32[]{:S(2)}) collective-permute-start(bf16[32,4096]{1,0:T(8,128)(2,1)S(1)} %constant_dynamic-update-slice_fusion.refs_0_), channel_id=1, source_target_pairs={{480,0},{0,32},{32,64},{64,96},{96,128},{128,160},{160,192},{192,2... | collective-permute-start | bytes 786440 | tf_op jit(solution)/shard_map/measures/ppermute | solution.py:142
  52.9 3.1 %collective-permute-start.5 = (bf16[16,4096]{1,0:T(8,128)(2,1)S(1)}, bf16[16,4096]{1,0:T(8,128)(2,1)S(1)}, u32[]{:S(2)}, u32[]{:S(2)}) collective-permute-start(bf16[16,4096]{1,0:T(8,128)(2,1)S(1)} %get-tuple-element.6), channel_id=1, source_target_pairs={{64,0},{96,32},{128,64},{160,96},{192,128},{224,160},{256,192},{28... | collective-permute-start | bytes 393224 | tf_op jit(solution)/shard_map/measures/ppermute | solution.py:142
  56.0 3.1 %collective-permute-start.6 = (bf16[16,4096]{1,0:T(8,128)(2,1)S(1)}, bf16[16,4096]{1,0:T(8,128)(2,1)S(1)}, u32[]{:S(2)}, u32[]{:S(2)}) collective-permute-start(bf16[16,4096]{1,0:T(8,128)(2,1)S(1)} %get-tuple-element.5), channel_id=1, source_target_pairs={{448,0},{480,32},{0,64},{32,96},{64,128},{96,160},{128,192},{160,2... | collective-permute-start | bytes 393224 | tf_op jit(solution)/shard_map/measures/ppermute | solution.py:142
  59.1 8.3 %all-to-all-done = bf16[32,64,1024]{2,1,0:T(8,128)(2,1)} async-done(((bf16[32,64,1024]{2,1,0:T(8,128)(2,1)}), bf16[32,64,1024]{2,1,0:T(8,128)(2,1)}, u32[]{:S(2)}, u32[]{:S(2)}) %all-to-all-start) | async-done | bytes 4194336 | tf_op jit(solution)/shard_map/tiles/all_to_all | solution.py:192
  67.4 0.1 broadcast_in_dim.52.ssp_ref
  67.5 7.2 %pick.1.impact_ref = f32[32,4096]{1,0:T(8,128)S(1)} custom-call(s32[4,16]{1,0:T(4,128)S(1)} %copy-done.3, s32[16]{0:T(128)S(1)} %copy-done.4, bf16[64,32,1024]{2,1,0:T(8,128)(2,1)} %bitcast.1.tiles_ref, s32[4,4096]{1,0:T(4,128)S(1)} %copy-done, f32[4,4096]{1,0:T(4,128)S(1)} %copy-done.1, f32[16,128]{1,0:T(8,128)S(1)} %pad.4.curves_ref, ...), custom_call_target="tpu_custom_call" | custom-call | flops 4294967296 | bytes 4194304 | tf_op jit(solution)/shard_map/pick/pallas_call | solution.py:197
  74.7 0.5 product.1
  75.3 13.9 %all_to_all.10 = f32[32,1,128]{2,1,0:T(1,128)S(1)} all-to-all(f32[32,1,128]{2,1,0:T(1,128)S(1)} %bitcast.6), channel_id=1, replica_groups=mesh['ev'=16,'asset'=32] {'asset'}, dimensions={0} | all-to-all | bytes 32768 | tf_op jit(solution)/shard_map/sums/all_to_all | solution.py:215
  89.2 0.6 reduce_sum.11
  (21 shorter events, 0.1 us)
Async XLA Ops:
  3.5 11.6 %copy-start.5 = (bf16[8,4096]{1,0:T(8,128)(2,1)S(1)}, bf16[8,4096]{1,0:T(8,128)(2,1)}, u32[]{:S(2)}) copy-start(bf16[8,4096]{1,0:T(8,128)(2,1)} %param.19) | copy-start | bytes 196612
  3.5 33.6 %copy-start.6 = (f32[16,16]{1,0:T(8,128)S(1)}, f32[16,16]{1,0:T(8,128)}, u32[]{:S(2)}) copy-start(f32[16,16]{1,0:T(8,128)} %param.16) | copy-start | bytes 3076
  3.6 63.8 %copy-start.7 = (s32[32]{0:T(128)S(1)}, s32[32]{0:T(128)}, u32[]{:S(2)}) copy-start(s32[32]{0:T(128)} %param.18) | copy-start | bytes 388
  3.6 63.9 %copy-start = (s32[4,4096]{1,0:T(4,128)S(1)}, s32[4,4096]{1,0:T(4,128)}, u32[]{:S(2)}) copy-start(s32[4,4096]{1,0:T(4,128)} %cells_ref.1) | copy-start | bytes 196612
  3.6 63.9 %copy-start.1 = (f32[4,4096]{1,0:T(4,128)S(1)}, f32[4,4096]{1,0:T(4,128)}, u32[]{:S(2)}) copy-start(f32[4,4096]{1,0:T(4,128)} %weights_ref.1) | copy-start | bytes 196612
  3.6 63.9 %copy-start.2 = (f32[3,4096]{1,0:T(4,128)S(1)}, f32[3,4096]{1,0:T(4,128)}, u32[]{:S(2)}) copy-start(f32[3,4096]{1,0:T(4,128)} %exposure_ref.1) | copy-start | bytes 147460
  3.6 63.9 %copy-start.3 = (s32[4,16]{1,0:T(4,128)S(1)}, s32[4,16]{1,0:T(4,128)}, u32[]{:S(2)}) copy-start(s32[4,16]{1,0:T(4,128)} %slots_ref.1) | copy-start | bytes 772
  3.6 63.9 %copy-start.4 = (s32[16]{0:T(128)S(1)}, s32[16]{0:T(128)}, u32[]{:S(2)}) copy-start(s32[16]{0:T(128)} %class_ref.1) | copy-start | bytes 196
  3.6 63.8 %all-to-all-start = ((bf16[32,64,1024]{2,1,0:T(8,128)(2,1)}), bf16[32,64,1024]{2,1,0:T(8,128)(2,1)}, u32[]{:S(2)}, u32[]{:S(2)}) async-start(bf16[32,64,1024]{2,1,0:T(8,128)(2,1)} %bitcast.7), calls=%async_computation | async-start | bytes 8388608 | tf_op jit(solution)/shard_map/tiles/all_to_all | solution.py:192
  15.1 22.1 %collective-permute-start = (bf16[8,4096]{1,0:T(8,128)(2,1)S(1)}, bf16[8,4096]{1,0:T(8,128)(2,1)S(1)}, u32[]{:S(2)}, u32[]{:S(2)}) collective-permute-start(bf16[8,4096]{1,0:T(8,128)(2,1)S(1)} %copy-done.5), channel_id=1, source_target_pairs={{128,0},{160,32},{192,64},{224,96},{256,128},{288,160},{320,192},{... | collective-permute-start | bytes 196616 | tf_op jit(solution)/shard_map/measures/ppermute | solution.py:142
  24.9 14.0 %collective-permute-start.1 = (bf16[8,4096]{1,0:T(8,128)(2,1)S(1)}, bf16[8,4096]{1,0:T(8,128)(2,1)S(1)}, u32[]{:S(2)}, u32[]{:S(2)}) collective-permute-start(bf16[8,4096]{1,0:T(8,128)(2,1)S(1)} %copy-done.5), channel_id=1, source_target_pairs={{256,0},{288,32},{320,64},{352,96},{384,128},{416,160},{448,192},{... | collective-permute-start | bytes 196616 | tf_op jit(solution)/shard_map/measures/ppermute | solution.py:142
  29.8 12.9 %collective-permute-start.2 = (bf16[8,4096]{1,0:T(8,128)(2,1)S(1)}, bf16[8,4096]{1,0:T(8,128)(2,1)S(1)}, u32[]{:S(2)}, u32[]{:S(2)}) collective-permute-start(bf16[8,4096]{1,0:T(8,128)(2,1)S(1)} %copy-done.5), channel_id=1, source_target_pairs={{384,0},{416,32},{448,64},{480,96},{0,128},{32,160},{64,192},{96,2... | collective-permute-start | bytes 196616 | tf_op jit(solution)/shard_map/measures/ppermute | solution.py:142
  42.7 32.0 %collective-permute-start.3 = (bf16[32,4096]{1,0:T(8,128)(2,1)S(1)}, bf16[32,4096]{1,0:T(8,128)(2,1)S(1)}, u32[]{:S(2)}, u32[]{:S(2)}) collective-permute-start(bf16[32,4096]{1,0:T(8,128)(2,1)S(1)} %constant_dynamic-update-slice_fusion.refs_0_), channel_id=1, source_target_pairs={{32,0},{64,32},{96,64},{128,96},{160,128},{192,160},{224,192},{256... | collective-permute-start | bytes 786440 | tf_op jit(solution)/shard_map/measures/ppermute | solution.py:142
  51.0 23.8 %collective-permute-start.4 = (bf16[32,4096]{1,0:T(8,128)(2,1)S(1)}, bf16[32,4096]{1,0:T(8,128)(2,1)S(1)}, u32[]{:S(2)}, u32[]{:S(2)}) collective-permute-start(bf16[32,4096]{1,0:T(8,128)(2,1)S(1)} %constant_dynamic-update-slice_fusion.refs_0_), channel_id=1, source_target_pairs={{480,0},{0,32},{32,64},{64,96},{96,128},{128,160},{160,192},{192,2... | collective-permute-start | bytes 786440 | tf_op jit(solution)/shard_map/measures/ppermute | solution.py:142
  52.9 21.8 %collective-permute-start.5 = (bf16[16,4096]{1,0:T(8,128)(2,1)S(1)}, bf16[16,4096]{1,0:T(8,128)(2,1)S(1)}, u32[]{:S(2)}, u32[]{:S(2)}) collective-permute-start(bf16[16,4096]{1,0:T(8,128)(2,1)S(1)} %get-tuple-element.6), channel_id=1, source_target_pairs={{64,0},{96,32},{128,64},{160,96},{192,128},{224,160},{256,192},{28... | collective-permute-start | bytes 393224 | tf_op jit(solution)/shard_map/measures/ppermute | solution.py:142
  56.0 18.7 %collective-permute-start.6 = (bf16[16,4096]{1,0:T(8,128)(2,1)S(1)}, bf16[16,4096]{1,0:T(8,128)(2,1)S(1)}, u32[]{:S(2)}, u32[]{:S(2)}) collective-permute-start(bf16[16,4096]{1,0:T(8,128)(2,1)S(1)} %get-tuple-element.5), channel_id=1, source_target_pairs={{448,0},{480,32},{0,64},{32,96},{64,128},{96,160},{128,192},{160,2... | collective-permute-start | bytes 393224 | tf_op jit(solution)/shard_map/measures/ppermute | solution.py:142

commit v4 on v3

--- a/solution.py
+++ b/solution.py
@@ -9,6 +9,8 @@
 TILE = 1024
 BLOCK = 256
 OVL = 4
+CAP = 2
+CORES = 2
 CORNERS = 4
 SSPS = 3
 CLASSES = 16
@@ -19,7 +21,15 @@
 PACK = 16
 
 
+def turned(slot, slots):
+    inner = CORES * CAP
+    bits = ((slots // inner).bit_length() - 1) // 2
+    chip = slot >> (inner.bit_length() - 1)
+    return (((chip & ((1 << bits) - 1)) << bits) + (chip >> bits)) * inner + (slot & (inner - 1))
+
+
 def pack_kernel(routes_ref, tiles_ref, out_ref, route_ref, hazard_ref, first_sems, sems):
+    slots = out_ref.shape[0]
     route = pltpu.make_async_copy(routes_ref, route_ref, first_sems.at[0])
     hazard = pltpu.make_async_copy(tiles_ref, hazard_ref, first_sems.at[1])
     route.start()
@@ -28,7 +38,7 @@
     hazard.wait()
 
     def copy(slot):
-        first = pl.multiple_of(route_ref[0, slot] * TILE, TILE)
+        first = pl.multiple_of(route_ref[0, turned(slot, slots)] * TILE, TILE)
         return pltpu.make_async_copy(hazard_ref.at[:, pl.ds(first, TILE)], out_ref.at[slot], sems.at[slot])
 
     @pl.loop(0, out_ref.shape[0])
@@ -44,6 +54,7 @@
     slots_ref, class_ref, tiles_ref, cells_ref, weights_ref, curves_ref, exposure_ref, ssp_ref, out_ref
 ):
     events = out_ref.shape[0]
+    slots = tiles_ref.shape[0]
     pieces = TILE // DEPTH
     groups = events // SUB
     rows = lax.broadcasted_iota(jnp.int32, (DEPTH, BLOCK), 0).astype(jnp.float32).astype(jnp.bfloat16)
@@ -60,7 +71,7 @@
     def _(block):
         assets = pl.ds(pl.multiple_of(block * BLOCK, BLOCK), BLOCK)
         window = [
-            tiles_ref[slots_ref[k, block], :, piece * DEPTH : (piece + 1) * DEPTH]
+            tiles_ref[turned(slots_ref[k, block], slots), :, piece * DEPTH : (piece + 1) * DEPTH]
             for k in range(OVL)
             for piece in range(pieces)
         ]
@@ -189,7 +200,9 @@
             cost_estimate=cost(0, 8 * slots * events * TILE),
         )(route_tiles, hazard)
     with jax.named_scope("tiles"):
-        tiles = lax.all_to_all(packed.reshape(devices, -1, TILE), "asset", 0, 0)
+        listed = [turned(CAP * device, slots) // CAP for device in range(devices)]
+        packed = packed.reshape(devices, -1, TILE)
+        tiles = lax.all_to_all(packed, "asset", 0, 0, axis_index_groups=[listed])
         tiles = tiles.reshape(slots, events, TILE)
     wide = jnp.pad(curves, ((0, 0), (0, LANES - LEVELS)))
     ssp = jnp.broadcast_to(event_ssp[:, None], (events, LANES))

time: 90.2 us -> 87.6 us (0.971)
  waiting for transfers between devices: 13.8 us -> 11.9 us
    all_to_all x1, waiting for transfers between devices: 8.29 us -> 6.49 us  [shards(): tiles = lax.all_to_all(packed, 'asset', 0, 0, axis_index_groups=[listed])]
where the time goes in v4:
time: 87.6 us; the launch traced here: 87.1 us
  starting transfers between devices  49.7 us (57%)
  blocking collectives  13.2 us (15%)
  waiting for transfers between devices  11.9 us (14%)
  Pallas kernels  11.3 us (13%)
    ppermute x7, starting transfers between devices, from_layer(): lax.ppermute(rows, 'ev', [((i + ahead) % layers, i) for i in range(layers)])  38.3 us
    all_to_all x1, blocking collectives, shards(): shares = lax.all_to_all(terms[:, None, :], 'asset', 0, 0)  13.2 us
    all_to_all x1, starting transfers between devices, shards(): tiles = lax.all_to_all(packed, 'asset', 0, 0, axis_index_groups=[listed])  11.5 us
    pallas_call x1, Pallas kernels, shards(): pl.pallas_call(pick_kernel, out_shape=jax.ShapeDtypeStruct((events, span)...  7.2 us
    all_to_all x1, waiting for transfers between devices, shards(): tiles = lax.all_to_all(packed, 'asset', 0, 0, axis_index_groups=[listed])  6.49 us
    ppermute x7, waiting for transfers between devices, from_layer(): lax.ppermute(rows, 'ev', [((i + ahead) % layers, i) for i in range(layers)])  5.44 us
    pallas_call x1, Pallas kernels, shards(): pl.pallas_call(pack_kernel, out_shape=pltpu.HBM((slots, events, TILE), jn...  3.52 us
  transfers between devices with their start and end apart: 8, of which 3 were waited for; matrix products, arithmetic and copies ran while one was open for 0% of the time, Pallas kernels for 8%

profile of v4, /device:TPU:1, one launch (start us, length us, event | category | flops | bytes accessed | tf_op | source)
XLA Modules:
  0.0 87.1 jit_solution(15960669394400378748)
XLA Ops:
  0.0 3.5 %pack.1 = bf16[64,32,1024]{2,1,0:T(8,128)(2,1)} custom-call(s32[1,64]{1,0:T(1,128)} %routes_ref.1, bf16[32,5120]{1,0:T(8,128)(2,1)} %tiles_ref.1), custom_call_target="tpu_custom_call" | custom-call | bytes 16777216 | tf_op jit(solution)/shard_map/pack/pallas_call | solution.py:189
  3.5 0.0 copy-start.5
  3.5 0.0 copy-start.6
  3.6 0.0 copy-start.7
  3.6 0.0 copy-start
  3.6 0.0 copy-start.1
  3.6 0.0 copy-start.3
  3.6 0.0 copy-start.4
  3.6 11.5 %all-to-all-start = ((bf16[32,64,1024]{2,1,0:T(8,128)(2,1)}), bf16[32,64,1024]{2,1,0:T(8,128)(2,1)}, u32[]{:S(2)}, u32[]{:S(2)}) async-start(bf16[32,64,1024]{2,1,0:T(8,128)(2,1)} %bitcast.7), calls=%async_computation | async-start | bytes 8388608 | tf_op jit(solution)/shard_map/tiles/all_to_all | solution.py:205
  15.1 9.8 %collective-permute-start = (bf16[8,4096]{1,0:T(8,128)(2,1)S(1)}, bf16[8,4096]{1,0:T(8,128)(2,1)S(1)}, u32[]{:S(2)}, u32[]{:S(2)}) collective-permute-start(bf16[8,4096]{1,0:T(8,128)(2,1)S(1)} %copy-done.5), channel_id=1, source_target_pairs={{128,0},{160,32},{192,64},{224,96},{256,128},{288,160},{320,192},{... | collective-permute-start | bytes 196616 | tf_op jit(solution)/shard_map/measures/ppermute | solution.py:153
  24.9 4.9 %collective-permute-start.1 = (bf16[8,4096]{1,0:T(8,128)(2,1)S(1)}, bf16[8,4096]{1,0:T(8,128)(2,1)S(1)}, u32[]{:S(2)}, u32[]{:S(2)}) collective-permute-start(bf16[8,4096]{1,0:T(8,128)(2,1)S(1)} %copy-done.5), channel_id=1, source_target_pairs={{256,0},{288,32},{320,64},{352,96},{384,128},{416,160},{448,192},{... | collective-permute-start | bytes 196616 | tf_op jit(solution)/shard_map/measures/ppermute | solution.py:153
  29.8 7.3 %collective-permute-start.2 = (bf16[8,4096]{1,0:T(8,128)(2,1)S(1)}, bf16[8,4096]{1,0:T(8,128)(2,1)S(1)}, u32[]{:S(2)}, u32[]{:S(2)}) collective-permute-start(bf16[8,4096]{1,0:T(8,128)(2,1)S(1)} %copy-done.5), channel_id=1, source_target_pairs={{384,0},{416,32},{448,64},{480,96},{0,128},{32,160},{64,192},{96,2... | collective-permute-start | bytes 196616 | tf_op jit(solution)/shard_map/measures/ppermute | solution.py:153
  37.2 1.8 %collective-permute-done.1 = bf16[8,4096]{1,0:T(8,128)(2,1)S(1)} collective-permute-done((bf16[8,4096]{1,0:T(8,128)(2,1)S(1)}, bf16[8,4096]{1,0:T(8,128)(2,1)S(1)}, u32[]{:S(2)}, u32[]{:S(2)}) %collective-permute-start.1) | collective-permute-done | bytes 65568 | tf_op jit(solution)/shard_map/measures/ppermute | solution.py:153
  39.0 3.7 %collective-permute-done.2 = bf16[8,4096]{1,0:T(8,128)(2,1)S(1)} collective-permute-done((bf16[8,4096]{1,0:T(8,128)(2,1)S(1)}, bf16[8,4096]{1,0:T(8,128)(2,1)S(1)}, u32[]{:S(2)}, u32[]{:S(2)}) %collective-permute-start.2) | collective-permute-done | bytes 65568 | tf_op jit(solution)/shard_map/measures/ppermute | solution.py:153
  42.6 8.2 %collective-permute-start.3 = (bf16[32,4096]{1,0:T(8,128)(2,1)S(1)}, bf16[32,4096]{1,0:T(8,128)(2,1)S(1)}, u32[]{:S(2)}, u32[]{:S(2)}) collective-permute-start(bf16[32,4096]{1,0:T(8,128)(2,1)S(1)} %constant_dynamic-update-slice_fusion.refs_0_), channel_id=1, source_target_pairs={{32,0},{64,32},{96,64},{128,96},{160,128},{192,160},{224,192},{256... | collective-permute-start | bytes 786440 | tf_op jit(solution)/shard_map/measures/ppermute | solution.py:153
  50.8 1.9 %collective-permute-start.4 = (bf16[32,4096]{1,0:T(8,128)(2,1)S(1)}, bf16[32,4096]{1,0:T(8,128)(2,1)S(1)}, u32[]{:S(2)}, u32[]{:S(2)}) collective-permute-start(bf16[32,4096]{1,0:T(8,128)(2,1)S(1)} %constant_dynamic-update-slice_fusion.refs_0_), channel_id=1, source_target_pairs={{480,0},{0,32},{32,64},{64,96},{96,128},{128,160},{160,192},{192,2... | collective-permute-start | bytes 786440 | tf_op jit(solution)/shard_map/measures/ppermute | solution.py:153
  52.8 3.1 %collective-permute-start.5 = (bf16[16,4096]{1,0:T(8,128)(2,1)S(1)}, bf16[16,4096]{1,0:T(8,128)(2,1)S(1)}, u32[]{:S(2)}, u32[]{:S(2)}) collective-permute-start(bf16[16,4096]{1,0:T(8,128)(2,1)S(1)} %get-tuple-element.6), channel_id=1, source_target_pairs={{64,0},{96,32},{128,64},{160,96},{192,128},{224,160},{256,192},{28... | collective-permute-start | bytes 393224 | tf_op jit(solution)/shard_map/measures/ppermute | solution.py:153
  55.9 3.1 %collective-permute-start.6 = (bf16[16,4096]{1,0:T(8,128)(2,1)S(1)}, bf16[16,4096]{1,0:T(8,128)(2,1)S(1)}, u32[]{:S(2)}, u32[]{:S(2)}) collective-permute-start(bf16[16,4096]{1,0:T(8,128)(2,1)S(1)} %get-tuple-element.5), channel_id=1, source_target_pairs={{448,0},{480,32},{0,64},{32,96},{64,128},{96,160},{128,192},{160,2... | collective-permute-start | bytes 393224 | tf_op jit(solution)/shard_map/measures/ppermute | solution.py:153
  59.0 6.5 %all-to-all-done = bf16[32,64,1024]{2,1,0:T(8,128)(2,1)} async-done(((bf16[32,64,1024]{2,1,0:T(8,128)(2,1)}), bf16[32,64,1024]{2,1,0:T(8,128)(2,1)}, u32[]{:S(2)}, u32[]{:S(2)}) %all-to-all-start) | async-done | bytes 4194336 | tf_op jit(solution)/shard_map/tiles/all_to_all | solution.py:205
  65.5 0.1 broadcast_in_dim.52.ssp_ref
  65.6 7.2 %pick.1.impact_ref = f32[32,4096]{1,0:T(8,128)S(1)} custom-call(s32[4,16]{1,0:T(4,128)S(1)} %copy-done.3, s32[16]{0:T(128)S(1)} %copy-done.4, bf16[64,32,1024]{2,1,0:T(8,128)(2,1)} %bitcast.1.tiles_ref, s32[4,4096]{1,0:T(4,128)S(1)} %copy-done, f32[4,4096]{1,0:T(4,128)S(1)} %copy-done.1, f32[16,128]{1,0:T(8,128)S(1)} %pad.4.curves_ref, ...), custom_call_target="tpu_custom_call" | custom-call | flops 4294967296 | bytes 4194304 | tf_op jit(solution)/shard_map/pick/pallas_call | solution.py:210
  72.8 0.5 product.1
  73.4 13.2 %all_to_all.10 = f32[32,1,128]{2,1,0:T(1,128)S(1)} all-to-all(f32[32,1,128]{2,1,0:T(1,128)S(1)} %bitcast.6), channel_id=1, replica_groups=mesh['ev'=16,'asset'=32] {'asset'}, dimensions={0} | all-to-all | bytes 32768 | tf_op jit(solution)/shard_map/sums/all_to_all | solution.py:228
  86.6 0.6 reduce_sum.11
  (21 shorter events, 0.1 us)
Async XLA Ops:
  3.5 11.6 %copy-start.5 = (bf16[8,4096]{1,0:T(8,128)(2,1)S(1)}, bf16[8,4096]{1,0:T(8,128)(2,1)}, u32[]{:S(2)}) copy-start(bf16[8,4096]{1,0:T(8,128)(2,1)} %param.19) | copy-start | bytes 196612
  3.5 33.6 %copy-start.6 = (f32[16,16]{1,0:T(8,128)S(1)}, f32[16,16]{1,0:T(8,128)}, u32[]{:S(2)}) copy-start(f32[16,16]{1,0:T(8,128)} %param.16) | copy-start | bytes 3076
  3.6 61.9 %copy-start.7 = (s32[32]{0:T(128)S(1)}, s32[32]{0:T(128)}, u32[]{:S(2)}) copy-start(s32[32]{0:T(128)} %param.18) | copy-start | bytes 388
  3.6 62.0 %copy-start = (s32[4,4096]{1,0:T(4,128)S(1)}, s32[4,4096]{1,0:T(4,128)}, u32[]{:S(2)}) copy-start(s32[4,4096]{1,0:T(4,128)} %cells_ref.1) | copy-start | bytes 196612
  3.6 62.0 %copy-start.1 = (f32[4,4096]{1,0:T(4,128)S(1)}, f32[4,4096]{1,0:T(4,128)}, u32[]{:S(2)}) copy-start(f32[4,4096]{1,0:T(4,128)} %weights_ref.1) | copy-start | bytes 196612
  3.6 62.0 %copy-start.2 = (f32[3,4096]{1,0:T(4,128)S(1)}, f32[3,4096]{1,0:T(4,128)}, u32[]{:S(2)}) copy-start(f32[3,4096]{1,0:T(4,128)} %exposure_ref.1) | copy-start | bytes 147460
  3.6 62.0 %copy-start.3 = (s32[4,16]{1,0:T(4,128)S(1)}, s32[4,16]{1,0:T(4,128)}, u32[]{:S(2)}) copy-start(s32[4,16]{1,0:T(4,128)} %slots_ref.1) | copy-start | bytes 772
  3.6 62.0 %copy-start.4 = (s32[16]{0:T(128)S(1)}, s32[16]{0:T(128)}, u32[]{:S(2)}) copy-start(s32[16]{0:T(128)} %class_ref.1) | copy-start | bytes 196
  3.6 61.9 %all-to-all-start = ((bf16[32,64,1024]{2,1,0:T(8,128)(2,1)}), bf16[32,64,1024]{2,1,0:T(8,128)(2,1)}, u32[]{:S(2)}, u32[]{:S(2)}) async-start(bf16[32,64,1024]{2,1,0:T(8,128)(2,1)} %bitcast.7), calls=%async_computation | async-start | bytes 8388608 | tf_op jit(solution)/shard_map/tiles/all_to_all | solution.py:205
  15.1 22.1 %collective-permute-start = (bf16[8,4096]{1,0:T(8,128)(2,1)S(1)}, bf16[8,4096]{1,0:T(8,128)(2,1)S(1)}, u32[]{:S(2)}, u32[]{:S(2)}) collective-permute-start(bf16[8,4096]{1,0:T(8,128)(2,1)S(1)} %copy-done.5), channel_id=1, source_target_pairs={{128,0},{160,32},{192,64},{224,96},{256,128},{288,160},{320,192},{... | collective-permute-start | bytes 196616 | tf_op jit(solution)/shard_map/measures/ppermute | solution.py:153
  24.9 14.0 %collective-permute-start.1 = (bf16[8,4096]{1,0:T(8,128)(2,1)S(1)}, bf16[8,4096]{1,0:T(8,128)(2,1)S(1)}, u32[]{:S(2)}, u32[]{:S(2)}) collective-permute-start(bf16[8,4096]{1,0:T(8,128)(2,1)S(1)} %copy-done.5), channel_id=1, source_target_pairs={{256,0},{288,32},{320,64},{352,96},{384,128},{416,160},{448,192},{... | collective-permute-start | bytes 196616 | tf_op jit(solution)/shard_map/measures/ppermute | solution.py:153
  29.8 12.8 %collective-permute-start.2 = (bf16[8,4096]{1,0:T(8,128)(2,1)S(1)}, bf16[8,4096]{1,0:T(8,128)(2,1)S(1)}, u32[]{:S(2)}, u32[]{:S(2)}) collective-permute-start(bf16[8,4096]{1,0:T(8,128)(2,1)S(1)} %copy-done.5), channel_id=1, source_target_pairs={{384,0},{416,32},{448,64},{480,96},{0,128},{32,160},{64,192},{96,2... | collective-permute-start | bytes 196616 | tf_op jit(solution)/shard_map/measures/ppermute | solution.py:153
  42.6 30.2 %collective-permute-start.3 = (bf16[32,4096]{1,0:T(8,128)(2,1)S(1)}, bf16[32,4096]{1,0:T(8,128)(2,1)S(1)}, u32[]{:S(2)}, u32[]{:S(2)}) collective-permute-start(bf16[32,4096]{1,0:T(8,128)(2,1)S(1)} %constant_dynamic-update-slice_fusion.refs_0_), channel_id=1, source_target_pairs={{32,0},{64,32},{96,64},{128,96},{160,128},{192,160},{224,192},{256... | collective-permute-start | bytes 786440 | tf_op jit(solution)/shard_map/measures/ppermute | solution.py:153
  50.8 22.0 %collective-permute-start.4 = (bf16[32,4096]{1,0:T(8,128)(2,1)S(1)}, bf16[32,4096]{1,0:T(8,128)(2,1)S(1)}, u32[]{:S(2)}, u32[]{:S(2)}) collective-permute-start(bf16[32,4096]{1,0:T(8,128)(2,1)S(1)} %constant_dynamic-update-slice_fusion.refs_0_), channel_id=1, source_target_pairs={{480,0},{0,32},{32,64},{64,96},{96,128},{128,160},{160,192},{192,2... | collective-permute-start | bytes 786440 | tf_op jit(solution)/shard_map/measures/ppermute | solution.py:153
  52.8 20.0 %collective-permute-start.5 = (bf16[16,4096]{1,0:T(8,128)(2,1)S(1)}, bf16[16,4096]{1,0:T(8,128)(2,1)S(1)}, u32[]{:S(2)}, u32[]{:S(2)}) collective-permute-start(bf16[16,4096]{1,0:T(8,128)(2,1)S(1)} %get-tuple-element.6), channel_id=1, source_target_pairs={{64,0},{96,32},{128,64},{160,96},{192,128},{224,160},{256,192},{28... | collective-permute-start | bytes 393224 | tf_op jit(solution)/shard_map/measures/ppermute | solution.py:153
  55.9 16.9 %collective-permute-start.6 = (bf16[16,4096]{1,0:T(8,128)(2,1)S(1)}, bf16[16,4096]{1,0:T(8,128)(2,1)S(1)}, u32[]{:S(2)}, u32[]{:S(2)}) collective-permute-start(bf16[16,4096]{1,0:T(8,128)(2,1)S(1)} %get-tuple-element.5), channel_id=1, source_target_pairs={{448,0},{480,32},{0,64},{32,96},{64,128},{96,160},{128,192},{160,2... | collective-permute-start | bytes 393224 | tf_op jit(solution)/shard_map/measures/ppermute | solution.py:153

commit v5 on v4

--- a/solution.py
+++ b/solution.py
@@ -67,7 +67,7 @@
         ]
         return jnp.concatenate(hits, axis=0)
 
-    @pl.loop(0, slots_ref.shape[1], unroll=8)
+    @pl.loop(0, slots_ref.shape[1], unroll=16)
     def _(block):
         assets = pl.ds(pl.multiple_of(block * BLOCK, BLOCK), BLOCK)
         window = [

time: 87.6 us -> 87.3 us (level)
  no operation moved by 1% of the time
where the time goes in v5:
time: 87.3 us; the launch traced here: 86.8 us
  starting transfers between devices  49.7 us (57%)
  blocking collectives  13.2 us (15%)
  waiting for transfers between devices  11.9 us (14%)
  Pallas kernels  10.9 us (12%)
    ppermute x7, starting transfers between devices, from_layer(): lax.ppermute(rows, 'ev', [((i + ahead) % layers, i) for i in range(layers)])  38.3 us
    all_to_all x1, blocking collectives, shards(): shares = lax.all_to_all(terms[:, None, :], 'asset', 0, 0)  13.2 us
    all_to_all x1, starting transfers between devices, shards(): tiles = lax.all_to_all(packed, 'asset', 0, 0, axis_index_groups=[listed])  11.5 us
    pallas_call x1, Pallas kernels, shards(): pl.pallas_call(pick_kernel, out_shape=jax.ShapeDtypeStruct((events, span)...  6.88 us
    all_to_all x1, waiting for transfers between devices, shards(): tiles = lax.all_to_all(packed, 'asset', 0, 0, axis_index_groups=[listed])  6.49 us
    ppermute x7, waiting for transfers between devices, from_layer(): lax.ppermute(rows, 'ev', [((i + ahead) % layers, i) for i in range(layers)])  5.44 us
    pallas_call x1, Pallas kernels, shards(): pl.pallas_call(pack_kernel, out_shape=pltpu.HBM((slots, events, TILE), jn...  3.52 us
  transfers between devices with their start and end apart: 8, of which 3 were waited for; matrix products, arithmetic and copies ran while one was open for 0% of the time, Pallas kernels for 8%

profile of v5, /device:TPU:1, one launch (start us, length us, event | category | flops | bytes accessed | tf_op | source)
XLA Modules:
  0.0 86.8 jit_solution(99519190384873896)
XLA Ops:
  0.0 3.5 %pack.1 = bf16[64,32,1024]{2,1,0:T(8,128)(2,1)} custom-call(s32[1,64]{1,0:T(1,128)} %routes_ref.1, bf16[32,5120]{1,0:T(8,128)(2,1)} %tiles_ref.1), custom_call_target="tpu_custom_call" | custom-call | bytes 16777216 | tf_op jit(solution)/shard_map/pack/pallas_call | solution.py:189
  3.5 0.0 copy-start.5
  3.5 0.0 copy-start.6
  3.6 0.0 copy-start.7
  3.6 0.0 copy-start
  3.6 0.0 copy-start.1
  3.6 0.0 copy-start.3
  3.6 0.0 copy-start.4
  3.6 11.5 %all-to-all-start = ((bf16[32,64,1024]{2,1,0:T(8,128)(2,1)}), bf16[32,64,1024]{2,1,0:T(8,128)(2,1)}, u32[]{:S(2)}, u32[]{:S(2)}) async-start(bf16[32,64,1024]{2,1,0:T(8,128)(2,1)} %bitcast.7), calls=%async_computation | async-start | bytes 8388608 | tf_op jit(solution)/shard_map/tiles/all_to_all | solution.py:205
  15.1 9.8 %collective-permute-start = (bf16[8,4096]{1,0:T(8,128)(2,1)S(1)}, bf16[8,4096]{1,0:T(8,128)(2,1)S(1)}, u32[]{:S(2)}, u32[]{:S(2)}) collective-permute-start(bf16[8,4096]{1,0:T(8,128)(2,1)S(1)} %copy-done.5), channel_id=1, source_target_pairs={{128,0},{160,32},{192,64},{224,96},{256,128},{288,160},{320,192},{... | collective-permute-start | bytes 196616 | tf_op jit(solution)/shard_map/measures/ppermute | solution.py:153
  24.9 4.9 %collective-permute-start.1 = (bf16[8,4096]{1,0:T(8,128)(2,1)S(1)}, bf16[8,4096]{1,0:T(8,128)(2,1)S(1)}, u32[]{:S(2)}, u32[]{:S(2)}) collective-permute-start(bf16[8,4096]{1,0:T(8,128)(2,1)S(1)} %copy-done.5), channel_id=1, source_target_pairs={{256,0},{288,32},{320,64},{352,96},{384,128},{416,160},{448,192},{... | collective-permute-start | bytes 196616 | tf_op jit(solution)/shard_map/measures/ppermute | solution.py:153
  29.8 7.3 %collective-permute-start.2 = (bf16[8,4096]{1,0:T(8,128)(2,1)S(1)}, bf16[8,4096]{1,0:T(8,128)(2,1)S(1)}, u32[]{:S(2)}, u32[]{:S(2)}) collective-permute-start(bf16[8,4096]{1,0:T(8,128)(2,1)S(1)} %copy-done.5), channel_id=1, source_target_pairs={{384,0},{416,32},{448,64},{480,96},{0,128},{32,160},{64,192},{96,2... | collective-permute-start | bytes 196616 | tf_op jit(solution)/shard_map/measures/ppermute | solution.py:153
  37.2 1.8 %collective-permute-done.1 = bf16[8,4096]{1,0:T(8,128)(2,1)S(1)} collective-permute-done((bf16[8,4096]{1,0:T(8,128)(2,1)S(1)}, bf16[8,4096]{1,0:T(8,128)(2,1)S(1)}, u32[]{:S(2)}, u32[]{:S(2)}) %collective-permute-start.1) | collective-permute-done | bytes 65568 | tf_op jit(solution)/shard_map/measures/ppermute | solution.py:153
  39.0 3.7 %collective-permute-done.2 = bf16[8,4096]{1,0:T(8,128)(2,1)S(1)} collective-permute-done((bf16[8,4096]{1,0:T(8,128)(2,1)S(1)}, bf16[8,4096]{1,0:T(8,128)(2,1)S(1)}, u32[]{:S(2)}, u32[]{:S(2)}) %collective-permute-start.2) | collective-permute-done | bytes 65568 | tf_op jit(solution)/shard_map/measures/ppermute | solution.py:153
  42.6 8.2 %collective-permute-start.3 = (bf16[32,4096]{1,0:T(8,128)(2,1)S(1)}, bf16[32,4096]{1,0:T(8,128)(2,1)S(1)}, u32[]{:S(2)}, u32[]{:S(2)}) collective-permute-start(bf16[32,4096]{1,0:T(8,128)(2,1)S(1)} %constant_dynamic-update-slice_fusion.refs_0_), channel_id=1, source_target_pairs={{32,0},{64,32},{96,64},{128,96},{160,128},{192,160},{224,192},{256... | collective-permute-start | bytes 786440 | tf_op jit(solution)/shard_map/measures/ppermute | solution.py:153
  50.8 1.9 %collective-permute-start.4 = (bf16[32,4096]{1,0:T(8,128)(2,1)S(1)}, bf16[32,4096]{1,0:T(8,128)(2,1)S(1)}, u32[]{:S(2)}, u32[]{:S(2)}) collective-permute-start(bf16[32,4096]{1,0:T(8,128)(2,1)S(1)} %constant_dynamic-update-slice_fusion.refs_0_), channel_id=1, source_target_pairs={{480,0},{0,32},{32,64},{64,96},{96,128},{128,160},{160,192},{192,2... | collective-permute-start | bytes 786440 | tf_op jit(solution)/shard_map/measures/ppermute | solution.py:153
  52.8 3.1 %collective-permute-start.5 = (bf16[16,4096]{1,0:T(8,128)(2,1)S(1)}, bf16[16,4096]{1,0:T(8,128)(2,1)S(1)}, u32[]{:S(2)}, u32[]{:S(2)}) collective-permute-start(bf16[16,4096]{1,0:T(8,128)(2,1)S(1)} %get-tuple-element.6), channel_id=1, source_target_pairs={{64,0},{96,32},{128,64},{160,96},{192,128},{224,160},{256,192},{28... | collective-permute-start | bytes 393224 | tf_op jit(solution)/shard_map/measures/ppermute | solution.py:153
  55.9 3.1 %collective-permute-start.6 = (bf16[16,4096]{1,0:T(8,128)(2,1)S(1)}, bf16[16,4096]{1,0:T(8,128)(2,1)S(1)}, u32[]{:S(2)}, u32[]{:S(2)}) collective-permute-start(bf16[16,4096]{1,0:T(8,128)(2,1)S(1)} %get-tuple-element.5), channel_id=1, source_target_pairs={{448,0},{480,32},{0,64},{32,96},{64,128},{96,160},{128,192},{160,2... | collective-permute-start | bytes 393224 | tf_op jit(solution)/shard_map/measures/ppermute | solution.py:153
  59.0 6.5 %all-to-all-done = bf16[32,64,1024]{2,1,0:T(8,128)(2,1)} async-done(((bf16[32,64,1024]{2,1,0:T(8,128)(2,1)}), bf16[32,64,1024]{2,1,0:T(8,128)(2,1)}, u32[]{:S(2)}, u32[]{:S(2)}) %all-to-all-start) | async-done | bytes 4194336 | tf_op jit(solution)/shard_map/tiles/all_to_all | solution.py:205
  65.5 0.1 broadcast_in_dim.52.ssp_ref
  65.6 6.9 %pick.1.impact_ref = f32[32,4096]{1,0:T(8,128)S(1)} custom-call(s32[4,16]{1,0:T(4,128)S(1)} %copy-done.3, s32[16]{0:T(128)S(1)} %copy-done.4, bf16[64,32,1024]{2,1,0:T(8,128)(2,1)} %bitcast.1.tiles_ref, s32[4,4096]{1,0:T(4,128)S(1)} %copy-done, f32[4,4096]{1,0:T(4,128)S(1)} %copy-done.1, f32[16,128]{1,0:T(8,128)S(1)} %pad.4.curves_ref, ...), custom_call_target="tpu_custom_call" | custom-call | flops 4294967296 | bytes 4194304 | tf_op jit(solution)/shard_map/pick/pallas_call | solution.py:210
  72.5 0.5 product.1
  73.1 13.2 %all_to_all.10 = f32[32,1,128]{2,1,0:T(1,128)S(1)} all-to-all(f32[32,1,128]{2,1,0:T(1,128)S(1)} %bitcast.6), channel_id=1, replica_groups=mesh['ev'=16,'asset'=32] {'asset'}, dimensions={0} | all-to-all | bytes 32768 | tf_op jit(solution)/shard_map/sums/all_to_all | solution.py:228
  86.3 0.6 reduce_sum.11
  (21 shorter events, 0.1 us)
Async XLA Ops:
  3.5 11.6 %copy-start.5 = (bf16[8,4096]{1,0:T(8,128)(2,1)S(1)}, bf16[8,4096]{1,0:T(8,128)(2,1)}, u32[]{:S(2)}) copy-start(bf16[8,4096]{1,0:T(8,128)(2,1)} %param.19) | copy-start | bytes 196612
  3.5 33.6 %copy-start.6 = (f32[16,16]{1,0:T(8,128)S(1)}, f32[16,16]{1,0:T(8,128)}, u32[]{:S(2)}) copy-start(f32[16,16]{1,0:T(8,128)} %param.16) | copy-start | bytes 3076
  3.6 61.9 %copy-start.7 = (s32[32]{0:T(128)S(1)}, s32[32]{0:T(128)}, u32[]{:S(2)}) copy-start(s32[32]{0:T(128)} %param.18) | copy-start | bytes 388
  3.6 62.0 %copy-start = (s32[4,4096]{1,0:T(4,128)S(1)}, s32[4,4096]{1,0:T(4,128)}, u32[]{:S(2)}) copy-start(s32[4,4096]{1,0:T(4,128)} %cells_ref.1) | copy-start | bytes 196612
  3.6 62.0 %copy-start.1 = (f32[4,4096]{1,0:T(4,128)S(1)}, f32[4,4096]{1,0:T(4,128)}, u32[]{:S(2)}) copy-start(f32[4,4096]{1,0:T(4,128)} %weights_ref.1) | copy-start | bytes 196612
  3.6 62.0 %copy-start.2 = (f32[3,4096]{1,0:T(4,128)S(1)}, f32[3,4096]{1,0:T(4,128)}, u32[]{:S(2)}) copy-start(f32[3,4096]{1,0:T(4,128)} %exposure_ref.1) | copy-start | bytes 147460
  3.6 62.0 %copy-start.3 = (s32[4,16]{1,0:T(4,128)S(1)}, s32[4,16]{1,0:T(4,128)}, u32[]{:S(2)}) copy-start(s32[4,16]{1,0:T(4,128)} %slots_ref.1) | copy-start | bytes 772
  3.6 62.0 %copy-start.4 = (s32[16]{0:T(128)S(1)}, s32[16]{0:T(128)}, u32[]{:S(2)}) copy-start(s32[16]{0:T(128)} %class_ref.1) | copy-start | bytes 196
  3.6 61.9 %all-to-all-start = ((bf16[32,64,1024]{2,1,0:T(8,128)(2,1)}), bf16[32,64,1024]{2,1,0:T(8,128)(2,1)}, u32[]{:S(2)}, u32[]{:S(2)}) async-start(bf16[32,64,1024]{2,1,0:T(8,128)(2,1)} %bitcast.7), calls=%async_computation | async-start | bytes 8388608 | tf_op jit(solution)/shard_map/tiles/all_to_all | solution.py:205
  15.1 22.1 %collective-permute-start = (bf16[8,4096]{1,0:T(8,128)(2,1)S(1)}, bf16[8,4096]{1,0:T(8,128)(2,1)S(1)}, u32[]{:S(2)}, u32[]{:S(2)}) collective-permute-start(bf16[8,4096]{1,0:T(8,128)(2,1)S(1)} %copy-done.5), channel_id=1, source_target_pairs={{128,0},{160,32},{192,64},{224,96},{256,128},{288,160},{320,192},{... | collective-permute-start | bytes 196616 | tf_op jit(solution)/shard_map/measures/ppermute | solution.py:153
  24.9 14.0 %collective-permute-start.1 = (bf16[8,4096]{1,0:T(8,128)(2,1)S(1)}, bf16[8,4096]{1,0:T(8,128)(2,1)S(1)}, u32[]{:S(2)}, u32[]{:S(2)}) collective-permute-start(bf16[8,4096]{1,0:T(8,128)(2,1)S(1)} %copy-done.5), channel_id=1, source_target_pairs={{256,0},{288,32},{320,64},{352,96},{384,128},{416,160},{448,192},{... | collective-permute-start | bytes 196616 | tf_op jit(solution)/shard_map/measures/ppermute | solution.py:153
  29.8 12.8 %collective-permute-start.2 = (bf16[8,4096]{1,0:T(8,128)(2,1)S(1)}, bf16[8,4096]{1,0:T(8,128)(2,1)S(1)}, u32[]{:S(2)}, u32[]{:S(2)}) collective-permute-start(bf16[8,4096]{1,0:T(8,128)(2,1)S(1)} %copy-done.5), channel_id=1, source_target_pairs={{384,0},{416,32},{448,64},{480,96},{0,128},{32,160},{64,192},{96,2... | collective-permute-start | bytes 196616 | tf_op jit(solution)/shard_map/measures/ppermute | solution.py:153
  42.6 29.9 %collective-permute-start.3 = (bf16[32,4096]{1,0:T(8,128)(2,1)S(1)}, bf16[32,4096]{1,0:T(8,128)(2,1)S(1)}, u32[]{:S(2)}, u32[]{:S(2)}) collective-permute-start(bf16[32,4096]{1,0:T(8,128)(2,1)S(1)} %constant_dynamic-update-slice_fusion.refs_0_), channel_id=1, source_target_pairs={{32,0},{64,32},{96,64},{128,96},{160,128},{192,160},{224,192},{256... | collective-permute-start | bytes 786440 | tf_op jit(solution)/shard_map/measures/ppermute | solution.py:153
  50.8 21.7 %collective-permute-start.4 = (bf16[32,4096]{1,0:T(8,128)(2,1)S(1)}, bf16[32,4096]{1,0:T(8,128)(2,1)S(1)}, u32[]{:S(2)}, u32[]{:S(2)}) collective-permute-start(bf16[32,4096]{1,0:T(8,128)(2,1)S(1)} %constant_dynamic-update-slice_fusion.refs_0_), channel_id=1, source_target_pairs={{480,0},{0,32},{32,64},{64,96},{96,128},{128,160},{160,192},{192,2... | collective-permute-start | bytes 786440 | tf_op jit(solution)/shard_map/measures/ppermute | solution.py:153
  52.8 19.7 %collective-permute-start.5 = (bf16[16,4096]{1,0:T(8,128)(2,1)S(1)}, bf16[16,4096]{1,0:T(8,128)(2,1)S(1)}, u32[]{:S(2)}, u32[]{:S(2)}) collective-permute-start(bf16[16,4096]{1,0:T(8,128)(2,1)S(1)} %get-tuple-element.6), channel_id=1, source_target_pairs={{64,0},{96,32},{128,64},{160,96},{192,128},{224,160},{256,192},{28... | collective-permute-start | bytes 393224 | tf_op jit(solution)/shard_map/measures/ppermute | solution.py:153
  55.9 16.6 %collective-permute-start.6 = (bf16[16,4096]{1,0:T(8,128)(2,1)S(1)}, bf16[16,4096]{1,0:T(8,128)(2,1)S(1)}, u32[]{:S(2)}, u32[]{:S(2)}) collective-permute-start(bf16[16,4096]{1,0:T(8,128)(2,1)S(1)} %get-tuple-element.5), channel_id=1, source_target_pairs={{448,0},{480,32},{0,64},{32,96},{64,128},{96,160},{128,192},{160,2... | collective-permute-start | bytes 393224 | tf_op jit(solution)/shard_map/measures/ppermute | solution.py:153

commit v6 on v3

--- a/solution.py
+++ b/solution.py
@@ -9,6 +9,7 @@
 TILE = 1024
 BLOCK = 256
 OVL = 4
+CAP = 2
 CORNERS = 4
 SSPS = 3
 CLASSES = 16
@@ -19,6 +20,14 @@
 PACK = 16
 
 
+def slot_at(place):
+    return ((place >> 1) & 3) * 16 + (place >> 4) * 4 + ((place >> 3) & 1) * 2 + (place & 1)
+
+
+def place_of(slot):
+    return ((slot >> 2) & 3) * 16 + ((slot >> 1) & 1) * 8 + (slot >> 4) * 2 + (slot & 1)
+
+
 def pack_kernel(routes_ref, tiles_ref, out_ref, route_ref, hazard_ref, first_sems, sems):
     route = pltpu.make_async_copy(routes_ref, route_ref, first_sems.at[0])
     hazard = pltpu.make_async_copy(tiles_ref, hazard_ref, first_sems.at[1])
@@ -28,7 +37,7 @@
     hazard.wait()
 
     def copy(slot):
-        first = pl.multiple_of(route_ref[0, slot] * TILE, TILE)
+        first = pl.multiple_of(route_ref[0, slot_at(slot)] * TILE, TILE)
         return pltpu.make_async_copy(hazard_ref.at[:, pl.ds(first, TILE)], out_ref.at[slot], sems.at[slot])
 
     @pl.loop(0, out_ref.shape[0])
@@ -56,11 +65,11 @@
         ]
         return jnp.concatenate(hits, axis=0)
 
-    @pl.loop(0, slots_ref.shape[1], unroll=8)
+    @pl.loop(0, slots_ref.shape[1], unroll=16)
     def _(block):
         assets = pl.ds(pl.multiple_of(block * BLOCK, BLOCK), BLOCK)
         window = [
-            tiles_ref[slots_ref[k, block], :, piece * DEPTH : (piece + 1) * DEPTH]
+            tiles_ref[place_of(slots_ref[k, block]), :, piece * DEPTH : (piece + 1) * DEPTH]
             for k in range(OVL)
             for piece in range(pieces)
         ]
@@ -189,7 +198,9 @@
             cost_estimate=cost(0, 8 * slots * events * TILE),
         )(route_tiles, hazard)
     with jax.named_scope("tiles"):
-        tiles = lax.all_to_all(packed.reshape(devices, -1, TILE), "asset", 0, 0)
+        listed = [slot_at(CAP * at) // CAP for at in range(devices)]
+        packed = packed.reshape(devices, -1, TILE)
+        tiles = lax.all_to_all(packed, "asset", 0, 0, axis_index_groups=[listed])
         tiles = tiles.reshape(slots, events, TILE)
     wide = jnp.pad(curves, ((0, 0), (0, LANES - LEVELS)))
     ssp = jnp.broadcast_to(event_ssp[:, None], (events, LANES))

time: 90.2 us -> 87 us (0.965)
  waiting for transfers between devices: 13.8 us -> 11.2 us
    all_to_all x1, waiting for transfers between devices: 8.29 us -> 5.76 us  [shards(): tiles = lax.all_to_all(packed, 'asset', 0, 0, axis_index_groups=[listed])]
where the time goes in v6:
time: 87 us; the launch traced here: 86.5 us
  starting transfers between devices  49.7 us (57%)
  blocking collectives  13.7 us (16%)
  waiting for transfers between devices  11.2 us (13%)
  Pallas kernels  10.9 us (13%)
    ppermute x7, starting transfers between devices, from_layer(): lax.ppermute(rows, 'ev', [((i + ahead) % layers, i) for i in range(layers)])  38.2 us
    all_to_all x1, blocking collectives, shards(): shares = lax.all_to_all(terms[:, None, :], 'asset', 0, 0)  13.7 us
    all_to_all x1, starting transfers between devices, shards(): tiles = lax.all_to_all(packed, 'asset', 0, 0, axis_index_groups=[listed])  11.5 us
    pallas_call x1, Pallas kernels, shards(): pl.pallas_call(pick_kernel, out_shape=jax.ShapeDtypeStruct((events, span)...  6.88 us
    all_to_all x1, waiting for transfers between devices, shards(): tiles = lax.all_to_all(packed, 'asset', 0, 0, axis_index_groups=[listed])  5.76 us
    ppermute x7, waiting for transfers between devices, from_layer(): lax.ppermute(rows, 'ev', [((i + ahead) % layers, i) for i in range(layers)])  5.44 us
    pallas_call x1, Pallas kernels, shards(): pl.pallas_call(pack_kernel, out_shape=pltpu.HBM((slots, events, TILE), jn...  3.52 us
  transfers between devices with their start and end apart: 8, of which 3 were waited for; matrix products, arithmetic and copies ran while one was open for 0% of the time, Pallas kernels for 8%

profile of v6, /device:TPU:1, one launch (start us, length us, event | category | flops | bytes accessed | tf_op | source)
XLA Modules:
  0.0 86.5 jit_solution(12674053129381144106)
XLA Ops:
  0.0 3.5 %pack.1 = bf16[64,32,1024]{2,1,0:T(8,128)(2,1)} custom-call(s32[1,64]{1,0:T(1,128)} %routes_ref.1, bf16[32,5120]{1,0:T(8,128)(2,1)} %tiles_ref.1), custom_call_target="tpu_custom_call" | custom-call | bytes 16777216 | tf_op jit(solution)/shard_map/pack/pallas_call | solution.py:187
  3.5 0.0 copy-start.5
  3.5 0.0 copy-start.6
  3.6 0.0 copy-start.7
  3.6 0.0 copy-start
  3.6 0.0 copy-start.1
  3.6 0.0 copy-start.2
  3.6 0.0 copy-start.3
  3.6 11.5 %all-to-all-start = ((bf16[32,64,1024]{2,1,0:T(8,128)(2,1)}), bf16[32,64,1024]{2,1,0:T(8,128)(2,1)}, u32[]{:S(2)}, u32[]{:S(2)}) async-start(bf16[32,64,1024]{2,1,0:T(8,128)(2,1)} %bitcast.7), calls=%async_computation | async-start | bytes 8388608 | tf_op jit(solution)/shard_map/tiles/all_to_all | solution.py:203
  15.1 9.8 %collective-permute-start = (bf16[8,4096]{1,0:T(8,128)(2,1)S(1)}, bf16[8,4096]{1,0:T(8,128)(2,1)S(1)}, u32[]{:S(2)}, u32[]{:S(2)}) collective-permute-start(bf16[8,4096]{1,0:T(8,128)(2,1)S(1)} %copy-done.5), channel_id=1, source_target_pairs={{128,0},{160,32},{192,64},{224,96},{256,128},{288,160},{320,192},{... | collective-permute-start | bytes 196616 | tf_op jit(solution)/shard_map/measures/ppermute | solution.py:151
  24.9 4.9 %collective-permute-start.1 = (bf16[8,4096]{1,0:T(8,128)(2,1)S(1)}, bf16[8,4096]{1,0:T(8,128)(2,1)S(1)}, u32[]{:S(2)}, u32[]{:S(2)}) collective-permute-start(bf16[8,4096]{1,0:T(8,128)(2,1)S(1)} %copy-done.5), channel_id=1, source_target_pairs={{256,0},{288,32},{320,64},{352,96},{384,128},{416,160},{448,192},{... | collective-permute-start | bytes 196616 | tf_op jit(solution)/shard_map/measures/ppermute | solution.py:151
  29.8 7.3 %collective-permute-start.2 = (bf16[8,4096]{1,0:T(8,128)(2,1)S(1)}, bf16[8,4096]{1,0:T(8,128)(2,1)S(1)}, u32[]{:S(2)}, u32[]{:S(2)}) collective-permute-start(bf16[8,4096]{1,0:T(8,128)(2,1)S(1)} %copy-done.5), channel_id=1, source_target_pairs={{384,0},{416,32},{448,64},{480,96},{0,128},{32,160},{64,192},{96,2... | collective-permute-start | bytes 196616 | tf_op jit(solution)/shard_map/measures/ppermute | solution.py:151
  37.2 1.8 %collective-permute-done.1 = bf16[8,4096]{1,0:T(8,128)(2,1)S(1)} collective-permute-done((bf16[8,4096]{1,0:T(8,128)(2,1)S(1)}, bf16[8,4096]{1,0:T(8,128)(2,1)S(1)}, u32[]{:S(2)}, u32[]{:S(2)}) %collective-permute-start.1) | collective-permute-done | bytes 65568 | tf_op jit(solution)/shard_map/measures/ppermute | solution.py:151
  39.0 3.7 %collective-permute-done.2 = bf16[8,4096]{1,0:T(8,128)(2,1)S(1)} collective-permute-done((bf16[8,4096]{1,0:T(8,128)(2,1)S(1)}, bf16[8,4096]{1,0:T(8,128)(2,1)S(1)}, u32[]{:S(2)}, u32[]{:S(2)}) %collective-permute-start.2) | collective-permute-done | bytes 65568 | tf_op jit(solution)/shard_map/measures/ppermute | solution.py:151
  42.6 8.2 %collective-permute-start.3 = (bf16[32,4096]{1,0:T(8,128)(2,1)S(1)}, bf16[32,4096]{1,0:T(8,128)(2,1)S(1)}, u32[]{:S(2)}, u32[]{:S(2)}) collective-permute-start(bf16[32,4096]{1,0:T(8,128)(2,1)S(1)} %constant_dynamic-update-slice_fusion.refs_0_), channel_id=1, source_target_pairs={{32,0},{64,32},{96,64},{128,96},{160,128},{192,160},{224,192},{256... | collective-permute-start | bytes 786440 | tf_op jit(solution)/shard_map/measures/ppermute | solution.py:151
  50.8 1.9 %collective-permute-start.4 = (bf16[32,4096]{1,0:T(8,128)(2,1)S(1)}, bf16[32,4096]{1,0:T(8,128)(2,1)S(1)}, u32[]{:S(2)}, u32[]{:S(2)}) collective-permute-start(bf16[32,4096]{1,0:T(8,128)(2,1)S(1)} %constant_dynamic-update-slice_fusion.refs_0_), channel_id=1, source_target_pairs={{480,0},{0,32},{32,64},{64,96},{96,128},{128,160},{160,192},{192,2... | collective-permute-start | bytes 786440 | tf_op jit(solution)/shard_map/measures/ppermute | solution.py:151
  52.8 3.1 %collective-permute-start.5 = (bf16[16,4096]{1,0:T(8,128)(2,1)S(1)}, bf16[16,4096]{1,0:T(8,128)(2,1)S(1)}, u32[]{:S(2)}, u32[]{:S(2)}) collective-permute-start(bf16[16,4096]{1,0:T(8,128)(2,1)S(1)} %get-tuple-element.6), channel_id=1, source_target_pairs={{64,0},{96,32},{128,64},{160,96},{192,128},{224,160},{256,192},{28... | collective-permute-start | bytes 393224 | tf_op jit(solution)/shard_map/measures/ppermute | solution.py:151
  55.9 3.1 %collective-permute-start.6 = (bf16[16,4096]{1,0:T(8,128)(2,1)S(1)}, bf16[16,4096]{1,0:T(8,128)(2,1)S(1)}, u32[]{:S(2)}, u32[]{:S(2)}) collective-permute-start(bf16[16,4096]{1,0:T(8,128)(2,1)S(1)} %get-tuple-element.5), channel_id=1, source_target_pairs={{448,0},{480,32},{0,64},{32,96},{64,128},{96,160},{128,192},{160,2... | collective-permute-start | bytes 393224 | tf_op jit(solution)/shard_map/measures/ppermute | solution.py:151
  59.0 5.8 %all-to-all-done = bf16[32,64,1024]{2,1,0:T(8,128)(2,1)} async-done(((bf16[32,64,1024]{2,1,0:T(8,128)(2,1)}), bf16[32,64,1024]{2,1,0:T(8,128)(2,1)}, u32[]{:S(2)}, u32[]{:S(2)}) %all-to-all-start) | async-done | bytes 4194336 | tf_op jit(solution)/shard_map/tiles/all_to_all | solution.py:203
  64.8 0.1 broadcast_in_dim.52.ssp_ref
  64.9 6.9 %pick.1.impact_ref = f32[32,4096]{1,0:T(8,128)S(1)} custom-call(s32[4,16]{1,0:T(4,128)S(1)} %copy-done.3, s32[16]{0:T(128)S(1)} %copy-done.4, bf16[64,32,1024]{2,1,0:T(8,128)(2,1)} %bitcast.1.tiles_ref, s32[4,4096]{1,0:T(4,128)S(1)} %copy-done, f32[4,4096]{1,0:T(4,128)S(1)} %copy-done.1, f32[16,128]{1,0:T(8,128)S(1)} %pad.4.curves_ref, ...), custom_call_target="tpu_custom_call" | custom-call | flops 4294967296 | bytes 4194304 | tf_op jit(solution)/shard_map/pick/pallas_call | solution.py:208
  71.8 0.5 product.1
  72.3 13.7 %all_to_all.10 = f32[32,1,128]{2,1,0:T(1,128)S(1)} all-to-all(f32[32,1,128]{2,1,0:T(1,128)S(1)} %bitcast.6), channel_id=1, replica_groups=mesh['ev'=16,'asset'=32] {'asset'}, dimensions={0} | all-to-all | bytes 32768 | tf_op jit(solution)/shard_map/sums/all_to_all | solution.py:226
  86.0 0.6 reduce_sum.11
  (21 shorter events, 0.1 us)
Async XLA Ops:
  3.5 11.6 %copy-start.5 = (bf16[8,4096]{1,0:T(8,128)(2,1)S(1)}, bf16[8,4096]{1,0:T(8,128)(2,1)}, u32[]{:S(2)}) copy-start(bf16[8,4096]{1,0:T(8,128)(2,1)} %param.19) | copy-start | bytes 196612
  3.5 33.6 %copy-start.6 = (f32[16,16]{1,0:T(8,128)S(1)}, f32[16,16]{1,0:T(8,128)}, u32[]{:S(2)}) copy-start(f32[16,16]{1,0:T(8,128)} %param.16) | copy-start | bytes 3076
  3.6 61.2 %copy-start.7 = (s32[32]{0:T(128)S(1)}, s32[32]{0:T(128)}, u32[]{:S(2)}) copy-start(s32[32]{0:T(128)} %param.18) | copy-start | bytes 388
  3.6 61.3 %copy-start = (s32[4,4096]{1,0:T(4,128)S(1)}, s32[4,4096]{1,0:T(4,128)}, u32[]{:S(2)}) copy-start(s32[4,4096]{1,0:T(4,128)} %cells_ref.1) | copy-start | bytes 196612
  3.6 61.3 %copy-start.1 = (f32[4,4096]{1,0:T(4,128)S(1)}, f32[4,4096]{1,0:T(4,128)}, u32[]{:S(2)}) copy-start(f32[4,4096]{1,0:T(4,128)} %weights_ref.1) | copy-start | bytes 196612
  3.6 61.2 %copy-start.2 = (f32[3,4096]{1,0:T(4,128)S(1)}, f32[3,4096]{1,0:T(4,128)}, u32[]{:S(2)}) copy-start(f32[3,4096]{1,0:T(4,128)} %exposure_ref.1) | copy-start | bytes 147460
  3.6 61.2 %copy-start.3 = (s32[4,16]{1,0:T(4,128)S(1)}, s32[4,16]{1,0:T(4,128)}, u32[]{:S(2)}) copy-start(s32[4,16]{1,0:T(4,128)} %slots_ref.1) | copy-start | bytes 772
  3.6 61.2 %copy-start.4 = (s32[16]{0:T(128)S(1)}, s32[16]{0:T(128)}, u32[]{:S(2)}) copy-start(s32[16]{0:T(128)} %class_ref.1) | copy-start | bytes 196
  3.6 61.1 %all-to-all-start = ((bf16[32,64,1024]{2,1,0:T(8,128)(2,1)}), bf16[32,64,1024]{2,1,0:T(8,128)(2,1)}, u32[]{:S(2)}, u32[]{:S(2)}) async-start(bf16[32,64,1024]{2,1,0:T(8,128)(2,1)} %bitcast.7), calls=%async_computation | async-start | bytes 8388608 | tf_op jit(solution)/shard_map/tiles/all_to_all | solution.py:203
  15.1 22.0 %collective-permute-start = (bf16[8,4096]{1,0:T(8,128)(2,1)S(1)}, bf16[8,4096]{1,0:T(8,128)(2,1)S(1)}, u32[]{:S(2)}, u32[]{:S(2)}) collective-permute-start(bf16[8,4096]{1,0:T(8,128)(2,1)S(1)} %copy-done.5), channel_id=1, source_target_pairs={{128,0},{160,32},{192,64},{224,96},{256,128},{288,160},{320,192},{... | collective-permute-start | bytes 196616 | tf_op jit(solution)/shard_map/measures/ppermute | solution.py:151
  24.9 14.0 %collective-permute-start.1 = (bf16[8,4096]{1,0:T(8,128)(2,1)S(1)}, bf16[8,4096]{1,0:T(8,128)(2,1)S(1)}, u32[]{:S(2)}, u32[]{:S(2)}) collective-permute-start(bf16[8,4096]{1,0:T(8,128)(2,1)S(1)} %copy-done.5), channel_id=1, source_target_pairs={{256,0},{288,32},{320,64},{352,96},{384,128},{416,160},{448,192},{... | collective-permute-start | bytes 196616 | tf_op jit(solution)/shard_map/measures/ppermute | solution.py:151
  29.8 12.8 %collective-permute-start.2 = (bf16[8,4096]{1,0:T(8,128)(2,1)S(1)}, bf16[8,4096]{1,0:T(8,128)(2,1)S(1)}, u32[]{:S(2)}, u32[]{:S(2)}) collective-permute-start(bf16[8,4096]{1,0:T(8,128)(2,1)S(1)} %copy-done.5), channel_id=1, source_target_pairs={{384,0},{416,32},{448,64},{480,96},{0,128},{32,160},{64,192},{96,2... | collective-permute-start | bytes 196616 | tf_op jit(solution)/shard_map/measures/ppermute | solution.py:151
  42.6 29.1 %collective-permute-start.3 = (bf16[32,4096]{1,0:T(8,128)(2,1)S(1)}, bf16[32,4096]{1,0:T(8,128)(2,1)S(1)}, u32[]{:S(2)}, u32[]{:S(2)}) collective-permute-start(bf16[32,4096]{1,0:T(8,128)(2,1)S(1)} %constant_dynamic-update-slice_fusion.refs_0_), channel_id=1, source_target_pairs={{32,0},{64,32},{96,64},{128,96},{160,128},{192,160},{224,192},{256... | collective-permute-start | bytes 786440 | tf_op jit(solution)/shard_map/measures/ppermute | solution.py:151
  50.8 20.9 %collective-permute-start.4 = (bf16[32,4096]{1,0:T(8,128)(2,1)S(1)}, bf16[32,4096]{1,0:T(8,128)(2,1)S(1)}, u32[]{:S(2)}, u32[]{:S(2)}) collective-permute-start(bf16[32,4096]{1,0:T(8,128)(2,1)S(1)} %constant_dynamic-update-slice_fusion.refs_0_), channel_id=1, source_target_pairs={{480,0},{0,32},{32,64},{64,96},{96,128},{128,160},{160,192},{192,2... | collective-permute-start | bytes 786440 | tf_op jit(solution)/shard_map/measures/ppermute | solution.py:151
  52.8 18.9 %collective-permute-start.5 = (bf16[16,4096]{1,0:T(8,128)(2,1)S(1)}, bf16[16,4096]{1,0:T(8,128)(2,1)S(1)}, u32[]{:S(2)}, u32[]{:S(2)}) collective-permute-start(bf16[16,4096]{1,0:T(8,128)(2,1)S(1)} %get-tuple-element.6), channel_id=1, source_target_pairs={{64,0},{96,32},{128,64},{160,96},{192,128},{224,160},{256,192},{28... | collective-permute-start | bytes 393224 | tf_op jit(solution)/shard_map/measures/ppermute | solution.py:151
  55.9 15.9 %collective-permute-start.6 = (bf16[16,4096]{1,0:T(8,128)(2,1)S(1)}, bf16[16,4096]{1,0:T(8,128)(2,1)S(1)}, u32[]{:S(2)}, u32[]{:S(2)}) collective-permute-start(bf16[16,4096]{1,0:T(8,128)(2,1)S(1)} %get-tuple-element.5), channel_id=1, source_target_pairs={{448,0},{480,32},{0,64},{32,96},{64,128},{96,160},{128,192},{160,2... | collective-permute-start | bytes 393224 | tf_op jit(solution)/shard_map/measures/ppermute | solution.py:151
